TPU v7x, 32 devices: a whole 2x2x4 slice. The times are simulated.
32 devices in a mesh: narrow: 4 (over y, core), wide: 8 (over z, x).
Axes of the slice: x: 2, y: 2, z: 4, core: 2. Of those that a mesh axis runs over, the one named last changes fastest.
Arguments:
- adjoint_hat: float32 [3, 2, 256, 256, 256], P(None, None, 'wide', 'narrow'), may hold values from -3 to 3
- velocity_hat: float32 [3, 2, 256, 256, 256], P(None, None, 'wide', 'narrow'), may hold values from -3 to 3
Outputs:
- adjoint_next: float32 [3, 2, 256, 256, 256], P(None, None, 'wide', 'narrow')
All inputs are finite; a program needn't handle non-finite values.
Results may differ from a plain program's by a relative error of at most 0.00005.
Values sent between devices are 32-bit elements; how exact they have to be, the bound alone decides.
A program may use at most 256 MiB of HBM per device.

v0:
```python
import math

import jax
import jax.numpy as jnp
from jax import lax
from jax.sharding import PartitionSpec as P

NX = 512
NY = 256
NZ = 256
KX = 256


section_step = 0.25
viscous_rate = 0.05
highest = lax.Precision.HIGHEST


def phase_tables(modes, places, length):
    mode_index = jnp.arange(modes, dtype=jnp.int32)[:, None]
    place_index = jnp.arange(places, dtype=jnp.int32)[None, :]
    angle = 2.0 * math.pi / length * (mode_index * place_index % length).astype(jnp.float32)
    return (jnp.cos(angle), jnp.sin(angle))


def rotation_merged(cosine, sine_part):
    table = jnp.stack([jnp.stack([cosine, sine_part], 0), jnp.stack([-sine_part, cosine], 0)], 0)
    length = cosine.shape[0]
    return table.transpose(0, 2, 1, 3)


def signed_wave(count, start, length):
    number = jnp.arange(count, dtype=jnp.int32) + start
    return jnp.where(number < length // 2, number, number - length)


def contract(pattern, values, table):
    return jnp.einsum(pattern, values, table, precision=highest)


def cross_wave(waves, field):
    return jnp.stack(
        [
            waves[1] * field[2] - waves[2] * field[1],
            waves[2] * field[0] - waves[0] * field[2],
            waves[0] * field[1] - waves[1] * field[0],
        ],
        0,
    )


def to_physical(leading, tables):
    inverse_z, inverse_y, synth_x = (tables[0], tables[1], tables[2])
    fields, rows_k, rows_b, merged_z = leading.shape
    depth = contract("fkbq,qdm->mfkdb", leading, inverse_z.reshape(2 * NZ, 2, NZ))
    moved = lax.all_to_all(depth, "narrow", split_axis=0, concat_axis=4, tiled=True)
    planes = moved.shape[0]
    moved = moved.reshape(planes, fields, rows_k, 2 * NY)
    span = contract("mfkq,qej->mfjek", moved, inverse_y.reshape(2 * NY, 2, NY))
    moved = lax.all_to_all(span, "wide", split_axis=0, concat_axis=4, tiled=True)
    moved = moved.reshape(moved.shape[0], fields, NY, 2 * KX)
    return contract("mfjq,qx->mfjx", moved, synth_x)


def to_spectral(physical, tables):
    forward_y, forward_z, anal_x = (tables[3], tables[4], tables[5])
    planes, fields = (physical.shape[0], physical.shape[1])
    stacked = contract("zfyx,xck->kzfcy", physical, anal_x)
    moved = lax.all_to_all(stacked, "wide", split_axis=0, concat_axis=1, tiled=True)
    rows_k = moved.shape[0]
    moved = moved.reshape(rows_k, moved.shape[1], fields, 2 * NY)
    span = contract("kzfq,qdj->jkfdz", moved, forward_y.reshape(2 * NY, 2, NY))
    moved = lax.all_to_all(span, "narrow", split_axis=0, concat_axis=4, tiled=True)
    rows_j = moved.shape[0]
    moved = moved.reshape(rows_j, rows_k, fields, 2 * NZ)
    return contract("jkfq,qen->fekjn", moved, forward_z.reshape(2 * NZ, 2, NZ))


def cross_cells(first, second):
    return jnp.stack(
        [
            first[1] * second[2] - first[2] * second[1],
            first[2] * second[0] - first[0] * second[2],
            first[0] * second[1] - first[1] * second[0],
        ],
        1,
    )


def local(adjoint_hat, velocity_hat):
    rows_x = adjoint_hat.shape[2]
    rows_y = adjoint_hat.shape[3]
    number_x = (lax.axis_index("wide") * rows_x + jnp.arange(rows_x, dtype=jnp.int32))[
        :, None, None
    ]
    number_y = signed_wave(rows_y, lax.axis_index("narrow") * rows_y, NY)[None, :, None]
    number_z = signed_wave(NZ, 0, NZ)[None, None, :]
    waves = [
        2.0 * math.pi / NX * number_x.astype(jnp.float32),
        2.0 * math.pi / NY * number_y.astype(jnp.float32),
        2.0 * math.pi / NZ * number_z.astype(jnp.float32),
    ]
    norm_scale = 1.0 / math.sqrt(NX * NY * NZ)
    cosine_z, sine_z = phase_tables(NZ, NZ, NZ)
    cosine_y, sine_y = phase_tables(NY, NY, NY)
    cosine_x, sine_x = phase_tables(KX, NX, NX)
    weights = (
        jnp.where(jnp.arange(KX, dtype=jnp.int32) == 0, 1.0, 2.0).astype(jnp.float32)[:, None]
        * norm_scale
    )
    synth_x = jnp.stack([cosine_x * weights, -sine_x * weights], 0).reshape(2 * KX, NX)
    anal_x = jnp.stack([cosine_x * norm_scale, -sine_x * norm_scale], 0).transpose(2, 0, 1)
    tables = (
        rotation_merged(cosine_z, sine_z),
        rotation_merged(cosine_y, sine_y),
        synth_x,
        rotation_merged(cosine_y, -sine_y),
        rotation_merged(cosine_z, -sine_z),
        anal_x,
    )
    vorticity_hat = jnp.stack(
        [-cross_wave(waves, velocity_hat[:, 1]), cross_wave(waves, velocity_hat[:, 0])], 1
    )
    fields = jnp.concatenate([adjoint_hat, velocity_hat, vorticity_hat], 0)
    leading = fields.transpose(0, 2, 3, 1, 4).reshape(9, rows_x, rows_y, 2 * NZ)
    inverse_bounds = [(member, member + 1) for member in range(9)]
    forward_bounds = [(member, member + 1) for member in range(6)]
    physical = jnp.concatenate(
        [to_physical(leading[lower:upper], tables) for lower, upper in inverse_bounds], 1
    )
    adjoint_cells = [physical[:, 0], physical[:, 1], physical[:, 2]]
    velocity_cells = [physical[:, 3], physical[:, 4], physical[:, 5]]
    vorticity_cells = [physical[:, 6], physical[:, 7], physical[:, 8]]
    rotation = cross_cells(adjoint_cells, vorticity_cells)
    transport = cross_cells(velocity_cells, adjoint_cells)
    products = jnp.concatenate([rotation, transport], 1)
    spectra = jnp.concatenate(
        [to_spectral(products[:, lower:upper], tables) for lower, upper in forward_bounds], 0
    )
    first = spectra[0:3]
    second = spectra[3:6]
    conv_real = first[:, 0] - cross_wave(waves, second[:, 1])
    conv_imag = first[:, 1] + cross_wave(waves, second[:, 0])
    keep = (
        (3 * number_x < NX) & (3 * jnp.abs(number_y) < NY) & (3 * jnp.abs(number_z) < NZ)
    ).astype(jnp.float32)
    ksquare = waves[0] ** 2 + waves[1] ** 2 + waves[2] ** 2
    divisor = ksquare + (ksquare == 0).astype(jnp.float32)
    decay = jnp.exp(-viscous_rate * ksquare)
    projected = []
    for convect in (conv_real, conv_imag):
        along = (waves[0] * convect[0] + waves[1] * convect[1] + waves[2] * convect[2]) / divisor
        projected.append(
            keep * (convect - jnp.stack([waves[0] * along, waves[1] * along, waves[2] * along], 0))
        )
    projected = jnp.stack(projected, 1)
    return decay * (adjoint_hat + section_step * projected)


def solution(mesh):
    in_specs = (P(None, None, "wide", "narrow", None), P(None, None, "wide", "narrow", None))
    out_specs = P(None, None, "wide", "narrow", None)
    return jax.shard_map(local, mesh=mesh, in_specs=in_specs, out_specs=out_specs, check_vma=False)
```

profile of v0, /device:TPU:0, one launch (start us, length us, event | category | flops | bytes accessed | tf_op | source)
XLA Modules:
  0.0 2720.3 jit_solution(3454026389043779705)
XLA Ops:
  18.5 25.7 maximum_bitcast_fusion
  44.3 25.9 fusion.103
  669.5 34.4 %all-to-all-done.1 = f32[64,1,256,2,32]{2,4,3,1,0:T(8,128)} async-done(((f32[64,1,256,2,32]{2,4,3,1,0:T(8,128)}), f32[64,1,256,2,32]{2,4,3,1,0:T(8,128)}, u32[]{:S(2)}, u32[]{:S(2)}) %all-to-all-start.1) | async-done | bytes 4194336 | tf_op jit(solution)/shard_map/all_to_all | solution.py:60
  708.4 15.6 reduce.10
  768.3 33.2 %all-to-all-done.13 = f32[64,1,256,2,32]{2,4,3,1,0:T(8,128)} async-done(((f32[64,1,256,2,32]{2,4,3,1,0:T(8,128)}), f32[64,1,256,2,32]{2,4,3,1,0:T(8,128)}, u32[]{:S(2)}, u32[]{:S(2)}) %all-to-all-start.13) | async-done | bytes 4194336 | tf_op jit(solution)/shard_map/all_to_all | solution.py:60
  866.0 32.5 %all-to-all-done.7 = f32[64,1,256,2,32]{2,4,3,1,0:T(8,128)} async-done(((f32[64,1,256,2,32]{2,4,3,1,0:T(8,128)}), f32[64,1,256,2,32]{2,4,3,1,0:T(8,128)}, u32[]{:S(2)}, u32[]{:S(2)}) %all-to-all-start.7) | async-done | bytes 4194336 | tf_op jit(solution)/shard_map/all_to_all | solution.py:60
  962.7 33.0 %all-to-all-done.11 = f32[64,1,256,2,32]{2,4,3,1,0:T(8,128)} async-done(((f32[64,1,256,2,32]{2,4,3,1,0:T(8,128)}), f32[64,1,256,2,32]{2,4,3,1,0:T(8,128)}, u32[]{:S(2)}, u32[]{:S(2)}) %all-to-all-start.11) | async-done | bytes 4194336 | tf_op jit(solution)/shard_map/all_to_all | solution.py:60
  1000.2 15.6 reduce.12
  1060.2 32.6 %all-to-all-done.5 = f32[64,1,256,2,32]{2,4,3,1,0:T(8,128)} async-done(((f32[64,1,256,2,32]{2,4,3,1,0:T(8,128)}), f32[64,1,256,2,32]{2,4,3,1,0:T(8,128)}, u32[]{:S(2)}, u32[]{:S(2)}) %all-to-all-start.5) | async-done | bytes 4194336 | tf_op jit(solution)/shard_map/all_to_all | solution.py:60
  1157.3 32.6 %all-to-all-done.3 = f32[64,1,256,2,32]{2,4,3,1,0:T(8,128)} async-done(((f32[64,1,256,2,32]{2,4,3,1,0:T(8,128)}), f32[64,1,256,2,32]{2,4,3,1,0:T(8,128)}, u32[]{:S(2)}, u32[]{:S(2)}) %all-to-all-start.3) | async-done | bytes 4194336 | tf_op jit(solution)/shard_map/all_to_all | solution.py:60
  1254.0 32.9 %all-to-all-done.21 = f32[64,1,256,2,32]{2,4,3,1,0:T(8,128)} async-done(((f32[64,1,256,2,32]{2,4,3,1,0:T(8,128)}), f32[64,1,256,2,32]{2,4,3,1,0:T(8,128)}, u32[]{:S(2)}, u32[]{:S(2)}) %all-to-all-start.21) | async-done | bytes 4194336 | tf_op jit(solution)/shard_map/all_to_all | solution.py:60
  1291.5 15.6 reduce
  1351.4 32.6 %all-to-all-done.25 = f32[64,1,256,2,32]{2,4,3,1,0:T(8,128)} async-done(((f32[64,1,256,2,32]{2,4,3,1,0:T(8,128)}), f32[64,1,256,2,32]{2,4,3,1,0:T(8,128)}, u32[]{:S(2)}, u32[]{:S(2)}) %all-to-all-start.25) | async-done | bytes 4194336 | tf_op jit(solution)/shard_map/all_to_all | solution.py:60
  1444.3 36.8 %all-to-all-done.19 = f32[64,1,256,2,32]{2,4,3,1,0:T(8,128)} async-done(((f32[64,1,256,2,32]{2,4,3,1,0:T(8,128)}), f32[64,1,256,2,32]{2,4,3,1,0:T(8,128)}, u32[]{:S(2)}, u32[]{:S(2)}) %all-to-all-start.19) | async-done | bytes 4194336 | tf_op jit(solution)/shard_map/all_to_all | solution.py:60
  1518.1 60.2 %all-to-all-done.16 = f32[256,8,1,2,256]{4,1,3,2,0:T(8,128)} async-done(((f32[256,8,1,2,256]{4,1,3,2,0:T(8,128)}), f32[256,8,1,2,256]{4,1,3,2,0:T(8,128)}, u32[]{:S(2)}, u32[]{:S(2)}) %all-to-all-start.16) | async-done | bytes 4194336 | tf_op jit(solution)/shard_map/all_to_all | solution.py:69
  1598.4 77.0 %all-to-all-done.14 = f32[256,8,1,2,256]{4,1,3,2,0:T(8,128)} async-done(((f32[256,8,1,2,256]{4,1,3,2,0:T(8,128)}), f32[256,8,1,2,256]{4,1,3,2,0:T(8,128)}, u32[]{:S(2)}, u32[]{:S(2)}) %all-to-all-start.14) | async-done | bytes 4194336 | tf_op jit(solution)/shard_map/all_to_all | solution.py:69
  1711.6 60.8 %all-to-all-done.8 = f32[256,8,1,2,256]{4,1,3,2,0:T(8,128)} async-done(((f32[256,8,1,2,256]{4,1,3,2,0:T(8,128)}), f32[256,8,1,2,256]{4,1,3,2,0:T(8,128)}, u32[]{:S(2)}, u32[]{:S(2)}) %all-to-all-start.8) | async-done | bytes 4194336 | tf_op jit(solution)/shard_map/all_to_all | solution.py:69
  1799.4 70.2 %all-to-all-done.28 = f32[256,8,1,2,256]{4,1,3,2,0:T(8,128)} async-done(((f32[256,8,1,2,256]{4,1,3,2,0:T(8,128)}), f32[256,8,1,2,256]{4,1,3,2,0:T(8,128)}, u32[]{:S(2)}, u32[]{:S(2)}) %all-to-all-start.28) | async-done | bytes 4194336 | tf_op jit(solution)/shard_map/all_to_all | solution.py:69
  1889.6 77.1 %all-to-all-done.22 = f32[256,8,1,2,256]{4,1,3,2,0:T(8,128)} async-done(((f32[256,8,1,2,256]{4,1,3,2,0:T(8,128)}), f32[256,8,1,2,256]{4,1,3,2,0:T(8,128)}, u32[]{:S(2)}, u32[]{:S(2)}) %all-to-all-start.22) | async-done | bytes 4194336 | tf_op jit(solution)/shard_map/all_to_all | solution.py:69
  2000.7 63.3 %all-to-all-done.26 = f32[256,8,1,2,256]{4,1,3,2,0:T(8,128)} async-done(((f32[256,8,1,2,256]{4,1,3,2,0:T(8,128)}), f32[256,8,1,2,256]{4,1,3,2,0:T(8,128)}, u32[]{:S(2)}, u32[]{:S(2)}) %all-to-all-start.26) | async-done | bytes 4194336 | tf_op jit(solution)/shard_map/all_to_all | solution.py:69
  2098.0 19.3 all-to-all-done.17
  2151.4 19.2 all-to-all-done.15
  2204.8 19.2 all-to-all-done.29
  2258.4 19.2 all-to-all-done.23
  (338 shorter events, 1834.5 us)
Async XLA Ops:
  111.0 53.7 %all-to-all-start = ((f32[4,1,262144]{2,1,0:T(1,128)}), f32[4,1,262144]{2,1,0:T(1,128)}, u32[]{:S(2)}, u32[]{:S(2)}) async-start(f32[4,1,262144]{2,1,0:T(1,128)} %reshape.1113), calls=%async_computation | async-start | bytes 8388608 | tf_op jit(solution)/shard_map/all_to_all | solution.py:56
  271.2 53.5 %all-to-all-start.10 = ((f32[4,1,262144]{2,1,0:T(1,128)}), f32[4,1,262144]{2,1,0:T(1,128)}, u32[]{:S(2)}, u32[]{:S(2)}) async-start(f32[4,1,262144]{2,1,0:T(1,128)} %reshape.1129), calls=%async_computation.10 | async-start | bytes 8388608 | tf_op jit(solution)/shard_map/all_to_all | solution.py:56
  431.2 53.5 %all-to-all-start.20 = ((f32[4,1,262144]{2,1,0:T(1,128)}), f32[4,1,262144]{2,1,0:T(1,128)}, u32[]{:S(2)}, u32[]{:S(2)}) async-start(f32[4,1,262144]{2,1,0:T(1,128)} %reshape.1115), calls=%async_computation.20 | async-start | bytes 8388608 | tf_op jit(solution)/shard_map/all_to_all | solution.py:56
  537.9 65.4 %all-to-all-start.18 = ((f32[4,1,262144]{2,1,0:T(1,128)}), f32[4,1,262144]{2,1,0:T(1,128)}, u32[]{:S(2)}, u32[]{:S(2)}) async-start(f32[4,1,262144]{2,1,0:T(1,128)} %reshape.1121), calls=%async_computation.18 | async-start | bytes 8388608 | tf_op jit(solution)/shard_map/all_to_all | solution.py:56
  603.3 100.6 %all-to-all-start.1 = ((f32[64,1,256,2,32]{2,4,3,1,0:T(8,128)}), f32[64,1,256,2,32]{2,4,3,1,0:T(8,128)}, u32[]{:S(2)}, u32[]{:S(2)}) async-start(f32[64,1,256,2,32]{2,4,3,1,0:T(8,128)} %copy.165), calls=%async_computation.1 | async-start | bytes 8388608 | tf_op jit(solution)/shard_map/all_to_all | solution.py:60
  703.9 97.6 %all-to-all-start.13 = ((f32[64,1,256,2,32]{2,4,3,1,0:T(8,128)}), f32[64,1,256,2,32]{2,4,3,1,0:T(8,128)}, u32[]{:S(2)}, u32[]{:S(2)}) async-start(f32[64,1,256,2,32]{2,4,3,1,0:T(8,128)} %copy.199), calls=%async_computation.13 | async-start | bytes 8388608 | tf_op jit(solution)/shard_map/all_to_all | solution.py:60
  801.4 97.1 %all-to-all-start.7 = ((f32[64,1,256,2,32]{2,4,3,1,0:T(8,128)}), f32[64,1,256,2,32]{2,4,3,1,0:T(8,128)}, u32[]{:S(2)}, u32[]{:S(2)}) async-start(f32[64,1,256,2,32]{2,4,3,1,0:T(8,128)} %copy.183), calls=%async_computation.7 | async-start | bytes 8388608 | tf_op jit(solution)/shard_map/all_to_all | solution.py:60
  898.5 97.1 %all-to-all-start.11 = ((f32[64,1,256,2,32]{2,4,3,1,0:T(8,128)}), f32[64,1,256,2,32]{2,4,3,1,0:T(8,128)}, u32[]{:S(2)}, u32[]{:S(2)}) async-start(f32[64,1,256,2,32]{2,4,3,1,0:T(8,128)} %copy.193), calls=%async_computation.11 | async-start | bytes 8388608 | tf_op jit(solution)/shard_map/all_to_all | solution.py:60
  995.6 97.1 %all-to-all-start.5 = ((f32[64,1,256,2,32]{2,4,3,1,0:T(8,128)}), f32[64,1,256,2,32]{2,4,3,1,0:T(8,128)}, u32[]{:S(2)}, u32[]{:S(2)}) async-start(f32[64,1,256,2,32]{2,4,3,1,0:T(8,128)} %copy.177), calls=%async_computation.5 | async-start | bytes 8388608 | tf_op jit(solution)/shard_map/all_to_all | solution.py:60
  1092.7 97.1 %all-to-all-start.3 = ((f32[64,1,256,2,32]{2,4,3,1,0:T(8,128)}), f32[64,1,256,2,32]{2,4,3,1,0:T(8,128)}, u32[]{:S(2)}, u32[]{:S(2)}) async-start(f32[64,1,256,2,32]{2,4,3,1,0:T(8,128)} %copy.171), calls=%async_computation.3 | async-start | bytes 8388608 | tf_op jit(solution)/shard_map/all_to_all | solution.py:60
  1189.8 97.1 %all-to-all-start.21 = ((f32[64,1,256,2,32]{2,4,3,1,0:T(8,128)}), f32[64,1,256,2,32]{2,4,3,1,0:T(8,128)}, u32[]{:S(2)}, u32[]{:S(2)}) async-start(f32[64,1,256,2,32]{2,4,3,1,0:T(8,128)} %copy.219), calls=%async_computation.21 | async-start | bytes 8388608 | tf_op jit(solution)/shard_map/all_to_all | solution.py:60
  1286.9 97.1 %all-to-all-start.25 = ((f32[64,1,256,2,32]{2,4,3,1,0:T(8,128)}), f32[64,1,256,2,32]{2,4,3,1,0:T(8,128)}, u32[]{:S(2)}, u32[]{:S(2)}) async-start(f32[64,1,256,2,32]{2,4,3,1,0:T(8,128)} %copy.229), calls=%async_computation.25 | async-start | bytes 8388608 | tf_op jit(solution)/shard_map/all_to_all | solution.py:60
  1384.1 97.1 %all-to-all-start.19 = ((f32[64,1,256,2,32]{2,4,3,1,0:T(8,128)}), f32[64,1,256,2,32]{2,4,3,1,0:T(8,128)}, u32[]{:S(2)}, u32[]{:S(2)}) async-start(f32[64,1,256,2,32]{2,4,3,1,0:T(8,128)} %copy.213), calls=%async_computation.19 | async-start | bytes 8388608 | tf_op jit(solution)/shard_map/all_to_all | solution.py:60
  1481.2 97.1 %all-to-all-start.16 = ((f32[256,8,1,2,256]{4,1,3,2,0:T(8,128)}), f32[256,8,1,2,256]{4,1,3,2,0:T(8,128)}, u32[]{:S(2)}, u32[]{:S(2)}) async-start(f32[256,8,1,2,256]{4,1,3,2,0:T(8,128)} %copy.206), calls=%async_computation.16 | async-start | bytes 8388608 | tf_op jit(solution)/shard_map/all_to_all | solution.py:69
  1578.3 97.1 %all-to-all-start.14 = ((f32[256,8,1,2,256]{4,1,3,2,0:T(8,128)}), f32[256,8,1,2,256]{4,1,3,2,0:T(8,128)}, u32[]{:S(2)}, u32[]{:S(2)}) async-start(f32[256,8,1,2,256]{4,1,3,2,0:T(8,128)} %copy.202), calls=%async_computation.14 | async-start | bytes 8388608 | tf_op jit(solution)/shard_map/all_to_all | solution.py:69
  1675.4 97.1 %all-to-all-start.8 = ((f32[256,8,1,2,256]{4,1,3,2,0:T(8,128)}), f32[256,8,1,2,256]{4,1,3,2,0:T(8,128)}, u32[]{:S(2)}, u32[]{:S(2)}) async-start(f32[256,8,1,2,256]{4,1,3,2,0:T(8,128)} %copy.186), calls=%async_computation.8 | async-start | bytes 8388608 | tf_op jit(solution)/shard_map/all_to_all | solution.py:69
  1772.5 97.1 %all-to-all-start.28 = ((f32[256,8,1,2,256]{4,1,3,2,0:T(8,128)}), f32[256,8,1,2,256]{4,1,3,2,0:T(8,128)}, u32[]{:S(2)}, u32[]{:S(2)}) async-start(f32[256,8,1,2,256]{4,1,3,2,0:T(8,128)} %copy.236), calls=%async_computation.28 | async-start | bytes 8388608 | tf_op jit(solution)/shard_map/all_to_all | solution.py:69
  1869.6 97.1 %all-to-all-start.22 = ((f32[256,8,1,2,256]{4,1,3,2,0:T(8,128)}), f32[256,8,1,2,256]{4,1,3,2,0:T(8,128)}, u32[]{:S(2)}, u32[]{:S(2)}) async-start(f32[256,8,1,2,256]{4,1,3,2,0:T(8,128)} %copy.222), calls=%async_computation.22 | async-start | bytes 8388608 | tf_op jit(solution)/shard_map/all_to_all | solution.py:69
  1966.7 97.3 %all-to-all-start.26 = ((f32[256,8,1,2,256]{4,1,3,2,0:T(8,128)}), f32[256,8,1,2,256]{4,1,3,2,0:T(8,128)}, u32[]{:S(2)}, u32[]{:S(2)}) async-start(f32[256,8,1,2,256]{4,1,3,2,0:T(8,128)} %copy.232), calls=%async_computation.26 | async-start | bytes 8388608 | tf_op jit(solution)/shard_map/all_to_all | solution.py:69
  2117.3 53.4 %all-to-all-start.15 = ((f32[4,1,262144]{2,1,0:T(1,128)}), f32[4,1,262144]{2,1,0:T(1,128)}, u32[]{:S(2)}, u32[]{:S(2)}) async-start(f32[4,1,262144]{2,1,0:T(1,128)} %reshape.1137), calls=%async_computation.15 | async-start | bytes 8388608 | tf_op jit(solution)/shard_map/all_to_all | solution.py:73
  2170.6 53.4 %all-to-all-start.29 = ((f32[4,1,262144]{2,1,0:T(1,128)}), f32[4,1,262144]{2,1,0:T(1,128)}, u32[]{:S(2)}, u32[]{:S(2)}) async-start(f32[4,1,262144]{2,1,0:T(1,128)} %reshape.1119), calls=%async_computation.29 | async-start | bytes 8388608 | tf_op jit(solution)/shard_map/all_to_all | solution.py:73
  2224.0 53.6 %all-to-all-start.23 = ((f32[4,1,262144]{2,1,0:T(1,128)}), f32[4,1,262144]{2,1,0:T(1,128)}, u32[]{:S(2)}, u32[]{:S(2)}) async-start(f32[4,1,262144]{2,1,0:T(1,128)} %reshape.1127), calls=%async_computation.23 | async-start | bytes 8388608 | tf_op jit(solution)/shard_map/all_to_all | solution.py:73
  2277.6 84.1 %all-to-all-start.27 = ((f32[4,1,262144]{2,1,0:T(1,128)}), f32[4,1,262144]{2,1,0:T(1,128)}, u32[]{:S(2)}, u32[]{:S(2)}) async-start(f32[4,1,262144]{2,1,0:T(1,128)} %reshape.1125), calls=%async_computation.27 | async-start | bytes 8388608 | tf_op jit(solution)/shard_map/all_to_all | solution.py:73
  2361.7 242.3 %all-to-all-start.9 = ((f32[4,1,262144]{2,1,0:T(1,128)}), f32[4,1,262144]{2,1,0:T(1,128)}, u32[]{:S(2)}, u32[]{:S(2)}) async-start(f32[4,1,262144]{2,1,0:T(1,128)} %reshape.1139), calls=%async_computation.9 | async-start | bytes 8388608 | tf_op jit(solution)/shard_map/all_to_all | solution.py:73
  (47 other events, 870.4 us)
where the time goes:
time: 2740 us; the launch traced here: 2720 us
  local copies, waits for them, and re-layouts  997 us (36%)
  waiting for transfers between devices  838 us (31%)
  matrix products  388 us (14%)
  other arithmetic  349 us (13%)
  starting transfers between devices  148 us (5%)
    all_to_all x6, waiting for transfers between devices, to_spectral(): lax.all_to_all(stacked, 'wide', split_axis=0, concat_axis=1, tiled=True)  408 us
    dot_general x45, matrix products, contract(): return jnp.einsum(pattern, values, table, precision=highest)  388 us
    all_to_all x9, waiting for transfers between devices, to_physical(): lax.all_to_all(span, 'wide', split_axis=0, concat_axis=4, tiled=True)  301 us
    unnamed x112, local copies, waits for them, and re-layouts  278 us
    transpose x30, local copies, waits for them, and re-layouts, contract(): return jnp.einsum(pattern, values, table, precision=highest)  204 us
    another operation x24, local copies, waits for them, and re-layouts  201 us
    all_to_all x9, other arithmetic, to_physical(): lax.all_to_all(depth, 'narrow', split_axis=0, concat_axis=4, tiled=True)  139 us
    all_to_all x10, local copies, waits for them, and re-layouts, to_physical(): lax.all_to_all(depth, 'narrow', split_axis=0, concat_axis=4, tiled=True)  110 us
  transfers between devices with their start and end apart: 30, of which 27 were waited for; matrix products, arithmetic and copies ran while one was open for 55% of the time, Pallas kernels for 0%

commit v1 on v0

v1 whole, which is shorter than its diff:
```python
import functools
import math

import jax
import jax.numpy as jnp
import ml_dtypes
import numpy as np
from jax import lax
from jax.experimental import pallas as pl
from jax.experimental.pallas import tpu as pltpu
from jax.sharding import PartitionSpec as P

NX = 512
NY = 256
NZ = 256
KX = 256

section_step = 0.25
viscous_rate = 0.05
axes = ("wide", "narrow")
VMEM_LIMIT = 60 * 2**20


def signed(count):
    number = np.arange(count)
    return np.where(number < count // 2, number, number - count).astype(np.float64)


def phases(modes, places, length):
    angle = 2.0 * math.pi / length * (np.outer(np.arange(modes), np.arange(places)) % length)
    return np.cos(angle), np.sin(angle)


def split_table(table):
    table = np.asarray(table, np.float32)
    high = table.astype(ml_dtypes.bfloat16)
    low = (table - high.astype(np.float32)).astype(ml_dtypes.bfloat16)
    return np.stack([high, low], 0)


def split(value):
    high = value.astype(jnp.bfloat16)
    return high, (value - high.astype(jnp.float32)).astype(jnp.bfloat16)


def product(left, right, dims):
    def one(first, second):
        return lax.dot_general(first, second, (dims, ((), ())), preferred_element_type=jnp.float32)

    return one(left[1], right[0]) + one(left[0], right[1]) + one(left[0], right[0])


def table_parts(ref):
    return ref[0], ref[1]


PLAIN = ((1,), (0,))
BOTH_MINOR = ((1,), (1,))


def whole_spec(shape):
    return pl.BlockSpec(shape, lambda *_: (0,) * len(shape), pipeline_mode=pl.Buffered(1))


def params():
    return pltpu.CompilerParams(vmem_limit_bytes=VMEM_LIMIT)


def cost(flops, moved):
    return pl.CostEstimate(flops=int(flops), bytes_accessed=int(moved), transcendentals=0)


def depth_kernel(tables_count, by_owner, field_ref, *refs):
    tables, outs = refs[:tables_count], refs[tables_count:]
    for row in range(field_ref.shape[2]):
        real, imag = field_ref[0, 0, row], field_ref[0, 1, row]
        first = jnp.concatenate([real, imag], 0)
        second = jnp.concatenate([-imag, real], 0)
        rows = split(jnp.concatenate([first, second], 1))
        for table, out in zip(tables, outs):
            value = product(table_parts(table), rows, BOTH_MINOR)
            if by_owner:
                out[:, row] = value.reshape(out.shape[0], out.shape[2], out.shape[3])
            else:
                out[row] = value


def depth(field, member, tables, owners):
    rows_x, rows_y = field.shape[2], field.shape[3]
    block = NZ // owners
    lanes = 2 * rows_y
    tile = min(8, rows_x)
    by_owner = block % 8 == 0
    if by_owner:
        shape = (owners, rows_x, block, lanes)
        spec = pl.BlockSpec((owners, tile, block, lanes), lambda i: (0, i, 0, 0))
    else:
        shape = (rows_x, NZ, lanes)
        spec = pl.BlockSpec((tile, NZ, lanes), lambda i: (i, 0, 0))
    count = len(tables)
    outs = pl.pallas_call(
        functools.partial(depth_kernel, count, by_owner),
        grid=(rows_x // tile,),
        in_specs=[pl.BlockSpec((1, 2, tile, rows_y, NZ), lambda i: (member, 0, i, 0, 0))]
        + [whole_spec(t.shape) for t in tables],
        out_specs=[spec] * count,
        out_shape=[jax.ShapeDtypeStruct(shape, jnp.float32)] * count,
        compiler_params=params(),
        cost_estimate=cost(6.0 * count * rows_x * lanes * NZ * 2 * NZ, 4 * (count + 1) * rows_x * lanes * NZ),
        name="depth_synthesis",
    )(field, *tables)
    if not by_owner:
        outs = [o.reshape(rows_x, owners, block, lanes).transpose(1, 0, 2, 3) for o in outs]
    return outs


def exchange(value):
    return lax.all_to_all(value, axes, split_axis=0, concat_axis=0, tiled=True)


def plane_rows(ref, narrow, block, plane):
    owners, rows, lanes = ref.shape
    value = ref[:, pl.ds(plane, rows // block, stride=block), :]
    value = value.reshape(owners // narrow, narrow, rows // block, lanes)
    pieces = [value[:, n].reshape(KX, lanes) for n in range(narrow)]
    return split(jnp.concatenate(pieces, 1))


def stacked(value):
    return jnp.concatenate([value[:, :NY], value[:, NY:]], 0)


def times_i(value):
    return jnp.concatenate([-value[:, NY:], value[:, :NY]], 1)


def lines(value, synth):
    return product(table_parts(synth), split(stacked(value)), PLAIN)


def velocity_kernel(narrow, block, *refs):
    ux, uy, uz, dzux, dzuy, span, slope, synth = refs[:8]
    outs = refs[8:]
    plane = pl.program_id(0)
    wave = lax.broadcasted_iota(jnp.int32, (KX, 2 * NY), 0).astype(jnp.float32) * (2.0 * math.pi / NX)

    def rows(ref):
        return plane_rows(ref, narrow, block, plane)

    def to_y(value, table):
        return product(value, table_parts(table), PLAIN)

    rows_x = rows(ux)
    value_x = to_y(rows_x, span)
    outs[0][0] = lines(value_x, synth)
    value_y = to_y(rows(uy), span)
    outs[1][0] = lines(value_y, synth)
    rows_z = rows(uz)
    value_z = to_y(rows_z, span)
    outs[2][0] = lines(value_z, synth)
    outs[3][0] = lines(to_y(rows_z, slope) - to_y(rows(dzuy), span), synth)
    outs[4][0] = lines(to_y(rows(dzux), span) - wave * times_i(value_z), synth)
    outs[5][0] = lines(wave * times_i(value_y) - to_y(rows_x, slope), synth)


def adjoint_kernel(narrow, block, field, span, synth, out):
    rows = plane_rows(field, narrow, block, pl.program_id(0))
    out[0] = lines(product(rows, table_parts(span), PLAIN), synth)


def physical_call(kernel, name, fields, tables, count, narrow):
    owners, rows_x, block, lanes = fields[0].shape
    fields = [f.reshape(owners, rows_x * block, lanes) for f in fields]
    spec = pl.BlockSpec((1, NX, NY), lambda z: (z, 0, 0))
    return pl.pallas_call(
        functools.partial(kernel, narrow, block),
        grid=(block,),
        in_specs=[whole_spec(f.shape) for f in fields] + [whole_spec(t.shape) for t in tables],
        out_specs=[spec] * count,
        out_shape=[jax.ShapeDtypeStruct((block, NX, NY), jnp.float32)] * count,
        compiler_params=params(),
        cost_estimate=cost(12.0 * count * block * KX * 4 * NY * NY, 4 * 2 * count * block * NX * NY),
        name=name,
    )(*fields, *tables)


def analysis_kernel(kept, rows_x, narrow, *refs):
    a = [r[0] for r in refs[0:3]]
    u = [r[0] for r in refs[3:6]]
    o = [r[0] for r in refs[6:9]]
    anal, span, slope = refs[9:12]
    outs = refs[12:]
    wave = lax.broadcasted_iota(jnp.int32, (kept, 2 * NY), 0).astype(jnp.float32) * (2.0 * math.pi / NX)

    def cross(p, q, c):
        d, e = (c + 1) % 3, (c + 2) % 3
        return p[d] * q[e] - p[e] * q[d]

    def modes(cells):
        value = product(table_parts(anal), split(cells), PLAIN)
        return jnp.concatenate([value[:kept], value[kept:]], 1)

    def to_y(value, table):
        return product(split(value), table_parts(table), PLAIN)

    def store(out, value):
        lanes = value.shape[1] // narrow
        for w in range(kept // rows_x):
            for n in range(narrow):
                out[w * narrow + n, 0] = value[w * rows_x : (w + 1) * rows_x, n * lanes : (n + 1) * lanes]
        for d in range(kept // rows_x * narrow, out.shape[0]):
            out[d, 0] = jnp.zeros(out.shape[2:], jnp.float32)

    tx, ty, tz = [modes(cross(u, a, c)) for c in range(3)]
    store(outs[3], to_y(tx, span))
    store(outs[4], to_y(ty, span))
    store(outs[0], to_y(modes(cross(a, o, 0)), span) + to_y(tz, slope))
    store(outs[1], to_y(modes(cross(a, o, 1)) - wave * times_i(tz), span))
    store(outs[2], to_y(modes(cross(a, o, 2)) + wave * times_i(ty), span) - to_y(tx, slope))


def analysis(fields, tables, kept, rows_x, wide, narrow):
    block = fields[0].shape[0]
    owners = wide * narrow
    lanes = 2 * NY // narrow
    spec = pl.BlockSpec((1, NX, NY), lambda z: (z, 0, 0))
    out = pl.BlockSpec((owners, 1, rows_x, lanes), lambda z: (0, z, 0, 0))
    return pl.pallas_call(
        functools.partial(analysis_kernel, kept, rows_x, narrow),
        grid=(block,),
        in_specs=[spec] * 9 + [whole_spec(t.shape) for t in tables],
        out_specs=[out] * 5,
        out_shape=[jax.ShapeDtypeStruct((owners, block, rows_x, lanes), jnp.float32)] * 5,
        compiler_params=params(),
        cost_estimate=cost(6.0 * block * 13 * kept * 2 * NX * NY, 4 * 14 * block * NX * NY),
        name="products_and_analysis",
    )(*fields, *tables)


def final_kernel(*refs):
    spectra, adjoint, table, out = refs[:5], refs[5], refs[6], refs[7]
    tile, rows_y = adjoint.shape[2], adjoint.shape[3]
    first_x = lax.axis_index("wide") * (tile * pl.num_programs(0)) + pl.program_id(0) * tile
    shape = (rows_y, NZ)
    number_y = lax.broadcasted_iota(jnp.int32, shape, 0) + lax.axis_index("narrow") * rows_y
    number_y = jnp.where(number_y < NY // 2, number_y, number_y - NY)
    number_z = lax.broadcasted_iota(jnp.int32, shape, 1)
    number_z = jnp.where(number_z < NZ // 2, number_z, number_z - NZ)
    keep_yz = (3 * jnp.abs(number_y) < NY) & (3 * jnp.abs(number_z) < NZ)
    ky = number_y.astype(jnp.float32) * (2.0 * math.pi / NY)
    kz = number_z.astype(jnp.float32) * (2.0 * math.pi / NZ)
    for row in range(tile):
        parts = []
        for ref in spectra:
            flat = ref.reshape(NZ * tile, 2 * rows_y)
            cells = flat[pl.ds(row, NZ, stride=tile), :].T
            both = product(split(cells), table_parts(table), PLAIN)
            cosine, sine = both[:, :NZ], both[:, NZ:]
            parts.append((cosine[:rows_y] + sine[rows_y:], cosine[rows_y:] - sine[:rows_y]))
        number_x = jnp.full(shape, first_x + row, jnp.int32)
        kx = number_x.astype(jnp.float32) * (2.0 * math.pi / NX)
        ksquare = kx * kx + ky * ky + kz * kz
        inverse = 1.0 / (ksquare + (ksquare == 0).astype(jnp.float32))
        keep = (keep_yz & (3 * number_x < NX)).astype(jnp.float32) * section_step
        decay = jnp.exp(-viscous_rate * ksquare)
        a1, a2, a3, t1, t2 = parts
        real = (a1[0] + kz * t2[1], a2[0] - kz * t1[1], a3[0])
        imag = (a1[1] - kz * t2[0], a2[1] + kz * t1[0], a3[1])
        for part, conv in enumerate((real, imag)):
            along = (kx * conv[0] + ky * conv[1] + kz * conv[2]) * inverse
            for c, wave in enumerate((kx, ky, kz)):
                out[c, part, row] = decay * (adjoint[c, part, row] + keep * (conv[c] - wave * along))


def final(spectra, adjoint_hat, table):
    rows_x, rows_y = adjoint_hat.shape[2], adjoint_hat.shape[3]
    tile = min(8, rows_x)
    spectra = [s.reshape(NZ, rows_x, 2 * rows_y) for s in spectra]
    hat = pl.BlockSpec((3, 2, tile, rows_y, NZ), lambda i: (0, 0, i, 0, 0))
    return pl.pallas_call(
        final_kernel,
        grid=(rows_x // tile,),
        in_specs=[pl.BlockSpec((NZ, tile, 2 * rows_y), lambda i: (0, i, 0))] * 5 + [hat, whole_spec(table.shape)],
        out_specs=hat,
        out_shape=jax.ShapeDtypeStruct(adjoint_hat.shape, jnp.float32),
        compiler_params=params(),
        cost_estimate=cost(30.0 * rows_x * 2 * rows_y * NZ * 2 * NZ, 4 * 22 * rows_x * rows_y * NZ),
        name="depth_analysis_projection",
    )(*spectra, adjoint_hat, table)


def local(wide, narrow, adjoint_hat, velocity_hat):
    owners = wide * narrow
    rows_x, rows_y = adjoint_hat.shape[2], adjoint_hat.shape[3]
    kept = -(-(-(-NX // 3)) // rows_x) * rows_x
    scale = 1.0 / math.sqrt(NX * NY * NZ)
    cosine, sine = phases(NZ, NZ, NZ)
    wave_z = 2.0 * math.pi / NZ * signed(NZ)[None, :]
    depth_table = split_table(np.concatenate([cosine, sine], 1))
    depth_slope = split_table(np.concatenate([-wave_z * sine, wave_z * cosine], 1))
    final_table = split_table(np.concatenate([cosine, sine], 1))
    cosine, sine = phases(NY, NY, NY)
    wave_y = 2.0 * math.pi / NY * signed(NY)[:, None]

    def merged(real, imag):
        return np.stack([np.stack([real, imag], 1), np.stack([-imag, real], 1)], 0)

    def rows_first(real, imag):
        table = merged(real, imag).reshape(2, narrow, rows_y, 2, NY)
        return split_table(table.transpose(1, 0, 2, 3, 4).reshape(2 * NY, 2 * NY))

    def rows_last(real, imag):
        table = merged(real, imag).transpose(0, 3, 2, 1).reshape(2, NY, 2, narrow, rows_y)
        return split_table(table.transpose(0, 1, 3, 2, 4).reshape(2 * NY, 2 * NY))

    span = rows_first(cosine, sine)
    slope = rows_first(-wave_y * sine, wave_y * cosine)
    back_span = rows_last(cosine, -sine)
    back_slope = rows_last(wave_y * sine, wave_y * cosine)
    cosine, sine = phases(KX, NX, NX)
    weights = np.where(np.arange(KX) == 0, 1.0, 2.0)[:, None] * scale
    synth = split_table(np.concatenate([cosine * weights, -sine * weights], 0).T)
    anal = split_table(np.concatenate([cosine[:kept], -sine[:kept]], 0) * scale)

    ux, dzux = [exchange(v) for v in depth(velocity_hat, 0, [depth_table, depth_slope], owners)]
    uy, dzuy = [exchange(v) for v in depth(velocity_hat, 1, [depth_table, depth_slope], owners)]
    uz = exchange(depth(velocity_hat, 2, [depth_table], owners)[0])
    hats = [exchange(depth(adjoint_hat, c, [depth_table], owners)[0]) for c in range(3)]
    flow = physical_call(
        velocity_kernel, "velocity_lines", [ux, uy, uz, dzux, dzuy], [span, slope, synth], 6, narrow
    )
    adjoint = [
        physical_call(adjoint_kernel, "adjoint_lines", [hat], [span, synth], 1, narrow)[0] for hat in hats
    ]
    spectra = analysis(
        adjoint + list(flow), [anal, back_span, back_slope], kept, rows_x, wide, narrow
    )
    return final([exchange(s) for s in spectra], adjoint_hat, final_table)


def solution(mesh):
    spec = P(None, None, "wide", "narrow", None)
    return jax.shard_map(
        functools.partial(local, mesh.shape["wide"], mesh.shape["narrow"]),
        mesh=mesh,
        in_specs=(spec, spec),
        out_specs=spec,
        check_vma=False,
    )
```

time: 2740 us -> 1430 us (0.52)
  local copies, waits for them, and re-layouts: 997 us -> 0.02 us
  blocking collectives: 0 us -> 686 us
  matrix products: 388 us -> 0 us
  waiting for transfers between devices: 838 us -> 465 us
  other arithmetic: 349 us -> 0 us
  Pallas kernels: 0 us -> 245 us
  starting transfers between devices: 148 us -> 31.5 us
    all_to_all x0 -> x7, blocking collectives: none -> 686 us  [exchange(): return lax.all_to_all(value, axes, split_axis=0, concat_axis=0, tiled=True)]
    dot_general x45 -> x0, matrix products: 388 us -> none  [contract(): return jnp.einsum(pattern, values, table, precision=highest)]
    all_to_all x30 -> x6, waiting for transfers between devices: 838 us -> 465 us  [exchange(): return lax.all_to_all(value, axes, split_axis=0, concat_axis=0, tiled=True)]
    unnamed x112 -> x8, local copies, waits for them, and re-layouts: 278 us -> 0.02 us
    pallas_call x0 -> x12, Pallas kernels: none -> 245 us  [the longest x4 101 us: physical_call(): pl.pallas_call(functools.partial(kernel, narrow, block), grid=(block,), i...]
    all_to_all x15 -> x0, other arithmetic: 230 us -> none  [the longest x9 139 us: to_physical(): lax.all_to_all(depth, 'narrow', split_axis=0, concat_axis=4, tiled=True)]
    all_to_all x31 -> x0, local copies, waits for them, and re-layouts: 223 us -> none  [the longest x10 110 us: to_physical(): lax.all_to_all(depth, 'narrow', split_axis=0, concat_axis=4, tiled=True)]
    transpose x31 -> x0, local copies, waits for them, and re-layouts: 204 us -> none  [the longest x30 204 us: contract(): return jnp.einsum(pattern, values, table, precision=highest)]
  transfers between devices with their start and end apart: 30 -> 6, of which waited for: 27 -> 6; matrix products, arithmetic and copies ran while one was open for 55% -> 0% of each run, Pallas kernels for 0% -> 7%
where the time goes in v1:
time: 1430 us
  blocking collectives  686 us (48%)
  waiting for transfers between devices  465 us (33%)
  Pallas kernels  245 us (17%)
  starting transfers between devices  31.5 us (2%)
    all_to_all x7, blocking collectives, exchange(): return lax.all_to_all(value, axes, split_axis=0, concat_axis=0, tiled=True)  686 us
    all_to_all x6, waiting for transfers between devices, exchange(): return lax.all_to_all(value, axes, split_axis=0, concat_axis=0, tiled=True)  465 us
    pallas_call x4, Pallas kernels, physical_call(): pl.pallas_call(functools.partial(kernel, narrow, block), grid=(block,), i...  101 us
    pallas_call x6, Pallas kernels, depth(): pl.pallas_call(functools.partial(depth_kernel, count, by_owner), grid=(ro...  71.5 us
    pallas_call x1, Pallas kernels, analysis(): pl.pallas_call(functools.partial(analysis_kernel, kept, rows_x, narrow),...  45 us
    all_to_all x6, starting transfers between devices, exchange(): return lax.all_to_all(value, axes, split_axis=0, concat_axis=0, tiled=True)  31.5 us
  transfers between devices with their start and end apart: 6, of which 6 were waited for; matrix products, arithmetic and copies ran while one was open for 0% of the time, Pallas kernels for 7%

profile of v1, /device:TPU:0, one launch (start us, length us, event | category | flops | bytes accessed | tf_op | source)
XLA Modules:
  0.0 1428.1 jit_solution(939268844976083900)
XLA Ops:
  17.0 9.6 depth_synthesis.7
  26.6 84.8 %all-to-all-done.5 = f32[32,32,8,128]{3,2,1,0:T(8,128)} async-done(((f32[32,32,8,128]{3,2,1,0:T(8,128)}), f32[32,32,8,128]{3,2,1,0:T(8,128)}, u32[]{:S(2)}, u32[]{:S(2)}) %all-to-all-start.5) | async-done | bytes 4194336 | tf_op jit(solution)/shard_map/all_to_all | solution.py:118
  116.8 9.6 depth_synthesis.6
  126.3 84.8 %all-to-all-done.1 = f32[32,32,8,128]{3,2,1,0:T(8,128)} async-done(((f32[32,32,8,128]{3,2,1,0:T(8,128)}), f32[32,32,8,128]{3,2,1,0:T(8,128)}, u32[]{:S(2)}, u32[]{:S(2)}) %all-to-all-start.1) | async-done | bytes 4194336 | tf_op jit(solution)/shard_map/all_to_all | solution.py:118
  216.5 9.6 depth_synthesis.8
  226.1 84.8 %all-to-all-done = f32[32,32,8,128]{3,2,1,0:T(8,128)} async-done(((f32[32,32,8,128]{3,2,1,0:T(8,128)}), f32[32,32,8,128]{3,2,1,0:T(8,128)}, u32[]{:S(2)}, u32[]{:S(2)}) %all-to-all-start) | async-done | bytes 4194336 | tf_op jit(solution)/shard_map/all_to_all | solution.py:118
  316.3 16.6 %depth_synthesis.10 = (f32[32,32,8,128]{3,2,1,0:T(8,128)}, f32[32,32,8,128]{3,2,1,0:T(8,128)}) custom-call(f32[3,2,32,64,256]{4,3,2,1,0:T(8,128)} %field_ref.11, bf16[2,256,512]{2,1,0:T(8,128)(2,1)} %constant.16.clone.refs_0_.refs_6_, bf16[2,256,512]{2,1,0:T(8,128)(2,1)} %constant.17.clone.refs_1_), custom_call_target="tpu_custom_call" | custom-call | flops 6442450944 | bytes 12582912 | tf_op jit(solution)/shard_map/depth_synthesis/pallas_call | solution.py:101
  332.9 77.8 %all-to-all-done.2 = f32[32,32,8,128]{3,2,1,0:T(8,128)} async-done(((f32[32,32,8,128]{3,2,1,0:T(8,128)}), f32[32,32,8,128]{3,2,1,0:T(8,128)}, u32[]{:S(2)}, u32[]{:S(2)}) %all-to-all-start.2) | async-done | bytes 4194336 | tf_op jit(solution)/shard_map/all_to_all | solution.py:118
  410.7 99.0 %all_to_all.65 = f32[32,32,8,128]{3,2,1,0:T(8,128)} all-to-all(f32[32,32,8,128]{3,2,1,0:T(8,128)} %get-tuple-element.21), channel_id=1, replica_groups=mesh['narrow'=4,'wide'=8] {'wide','narrow'}, dimensions={0} | all-to-all | bytes 8388608 | tf_op jit(solution)/shard_map/all_to_all | solution.py:118
  513.5 16.6 %depth_synthesis.9 = (f32[32,32,8,128]{3,2,1,0:T(8,128)}, f32[32,32,8,128]{3,2,1,0:T(8,128)}) custom-call(f32[3,2,32,64,256]{4,3,2,1,0:T(8,128)} %field_ref.11, bf16[2,256,512]{2,1,0:T(8,128)(2,1)} %constant.16.clone.refs_0_.refs_6_, bf16[2,256,512]{2,1,0:T(8,128)(2,1)} %constant.17.clone.refs_1_), custom_call_target="tpu_custom_call" | custom-call | flops 6442450944 | bytes 12582912 | tf_op jit(solution)/shard_map/depth_synthesis/pallas_call | solution.py:101
  530.1 77.8 %all-to-all-done.7 = f32[32,32,8,128]{3,2,1,0:T(8,128)} async-done(((f32[32,32,8,128]{3,2,1,0:T(8,128)}), f32[32,32,8,128]{3,2,1,0:T(8,128)}, u32[]{:S(2)}, u32[]{:S(2)}) %all-to-all-start.7) | async-done | bytes 4194336 | tf_op jit(solution)/shard_map/all_to_all | solution.py:118
  607.9 99.0 %all_to_all.66 = f32[32,32,8,128]{3,2,1,0:T(8,128)} all-to-all(f32[32,32,8,128]{3,2,1,0:T(8,128)} %get-tuple-element.20), channel_id=1, replica_groups=mesh['narrow'=4,'wide'=8] {'wide','narrow'}, dimensions={0} | all-to-all | bytes 8388608 | tf_op jit(solution)/shard_map/all_to_all | solution.py:118
  711.0 12.9 adjoint_lines.4.refs_1_
  723.9 12.9 adjoint_lines.3.refs_0_
  736.8 12.9 adjoint_lines.5.refs_2_
  749.7 55.5 %all-to-all-done.6 = f32[32,32,8,128]{3,2,1,0:T(8,128)} async-done(((f32[32,32,8,128]{3,2,1,0:T(8,128)}), f32[32,32,8,128]{3,2,1,0:T(8,128)}, u32[]{:S(2)}, u32[]{:S(2)}) %all-to-all-start.6) | async-done | bytes 4194336 | tf_op jit(solution)/shard_map/all_to_all | solution.py:118
  805.2 62.2 %velocity_lines.1 = (f32[8,512,256]{2,1,0:T(8,128)}, f32[8,512,256]{2,1,0:T(8,128)}, f32[8,512,256]{2,1,0:T(8,128)}, f32[8,512,256]{2,1,0:T(8,128)}, f32[8,512,256]{2,1,0:T(8,128)}, /*index=5*/f32[8,512,256]{2,1,0:T(8,128)}) custom-call(f32[32,256,128]{2,1,0:T(8,128)} %bitcast.14, f32[32,256,128]{2,1,0:T(8,128)} %bitcast.13, ...), custom_call_target="tpu_custom_call" | custom-call | flops 38654705664 | bytes 50331648 | tf_op jit(solution)/shard_map/velocity_lines/pallas_call | solution.py:175
  867.5 45.0 %products_and_analysis.1 = (f32[32,8,32,128]{3,2,1,0:T(8,128)}, f32[32,8,32,128]{3,2,1,0:T(8,128)}, f32[32,8,32,128]{3,2,1,0:T(8,128)}, f32[32,8,32,128]{3,2,1,0:T(8,128)}, f32[32,8,32,128]{3,2,1,0:T(8,128)}) custom-call(f32[8,512,256]{2,1,0:T(8,128)} %adjoint_lines.3.refs_0_, f32[8,512,256]{2,1,0:T(8,128)} %adjoint_lines.4.refs_1_, ...), custom_call_target="tpu_custom_call" | custom-call | flops 31406948352 | bytes 58720256 | tf_op jit(solution)/shard_map/products_and_analysis/pallas_call | solution.py:228
  912.5 99.0 %all_to_all.67 = f32[32,8,32,128]{3,2,1,0:T(8,128)} all-to-all(f32[32,8,32,128]{3,2,1,0:T(8,128)} %get-tuple-element.30), channel_id=1, replica_groups=mesh['narrow'=4,'wide'=8] {'wide','narrow'}, dimensions={0} | all-to-all | bytes 8388608 | tf_op jit(solution)/shard_map/all_to_all | solution.py:118
  1011.5 97.3 %all_to_all.68 = f32[32,8,32,128]{3,2,1,0:T(8,128)} all-to-all(f32[32,8,32,128]{3,2,1,0:T(8,128)S(1)} %copy-done.3), channel_id=1, replica_groups=mesh['narrow'=4,'wide'=8] {'wide','narrow'}, dimensions={0} | all-to-all | bytes 8388608 | tf_op jit(solution)/shard_map/all_to_all | solution.py:118
  1108.8 97.3 %all_to_all.69 = f32[32,8,32,128]{3,2,1,0:T(8,128)} all-to-all(f32[32,8,32,128]{3,2,1,0:T(8,128)S(1)} %copy-done.2), channel_id=1, replica_groups=mesh['narrow'=4,'wide'=8] {'wide','narrow'}, dimensions={0} | all-to-all | bytes 8388608 | tf_op jit(solution)/shard_map/all_to_all | solution.py:118
  1206.0 97.3 %all_to_all.70 = f32[32,8,32,128]{3,2,1,0:T(8,128)} all-to-all(f32[32,8,32,128]{3,2,1,0:T(8,128)S(1)} %copy-done.1), channel_id=1, replica_groups=mesh['narrow'=4,'wide'=8] {'wide','narrow'}, dimensions={0} | all-to-all | bytes 8388608 | tf_op jit(solution)/shard_map/all_to_all | solution.py:118
  1303.3 97.3 %all_to_all.71 = f32[32,8,32,128]{3,2,1,0:T(8,128)} all-to-all(f32[32,8,32,128]{3,2,1,0:T(8,128)S(1)} %copy-done), channel_id=1, replica_groups=mesh['narrow'=4,'wide'=8] {'wide','narrow'}, dimensions={0} | all-to-all | bytes 8388608 | tf_op jit(solution)/shard_map/all_to_all | solution.py:118
  1400.6 27.5 %depth_analysis_projection.1 = f32[3,2,32,64,256]{4,3,2,1,0:T(8,128)} custom-call(f32[256,32,128]{2,1,0:T(8,128)} %bitcast.15, f32[256,32,128]{2,1,0:T(8,128)} %bitcast.16, f32[256,32,128]{2,1,0:T(8,128)} %bitcast.17, f32[256,32,128]{2,1,0:T(8,128)} %bitcast.18, f32[256,32,128]{2,1,0:T(8,128)} %bitcast.19, f32[3,2,32,64,256]{4,3,2,1,0:T(8,128)} %refs_5_.2, ...), custom_call_target="tpu_custom_call" | custom-call | flops 16106127360 | bytes 46137344 | tf_op jit(solution)/shard_map/depth_analysis_projection/pallas_call | solution.py:280
  (15 shorter events, 41.1 us)
Async XLA Ops:
  9.6 101.8 %all-to-all-start.5 = ((f32[32,32,8,128]{3,2,1,0:T(8,128)}), f32[32,32,8,128]{3,2,1,0:T(8,128)}, u32[]{:S(2)}, u32[]{:S(2)}) async-start(f32[32,32,8,128]{3,2,1,0:T(8,128)} %depth_synthesis.11), calls=%async_computation.5 | async-start | bytes 8388608 | tf_op jit(solution)/shard_map/all_to_all | solution.py:118
  111.4 99.8 %all-to-all-start.1 = ((f32[32,32,8,128]{3,2,1,0:T(8,128)}), f32[32,32,8,128]{3,2,1,0:T(8,128)}, u32[]{:S(2)}, u32[]{:S(2)}) async-start(f32[32,32,8,128]{3,2,1,0:T(8,128)} %depth_synthesis.7), calls=%async_computation.1 | async-start | bytes 8388608 | tf_op jit(solution)/shard_map/all_to_all | solution.py:118
  211.1 99.8 %all-to-all-start = ((f32[32,32,8,128]{3,2,1,0:T(8,128)}), f32[32,32,8,128]{3,2,1,0:T(8,128)}, u32[]{:S(2)}, u32[]{:S(2)}) async-start(f32[32,32,8,128]{3,2,1,0:T(8,128)} %depth_synthesis.6), calls=%async_computation | async-start | bytes 8388608 | tf_op jit(solution)/shard_map/all_to_all | solution.py:118
  310.9 99.8 %all-to-all-start.2 = ((f32[32,32,8,128]{3,2,1,0:T(8,128)}), f32[32,32,8,128]{3,2,1,0:T(8,128)}, u32[]{:S(2)}, u32[]{:S(2)}) async-start(f32[32,32,8,128]{3,2,1,0:T(8,128)} %depth_synthesis.8), calls=%async_computation.2 | async-start | bytes 8388608 | tf_op jit(solution)/shard_map/all_to_all | solution.py:118
  509.7 98.2 %all-to-all-start.7 = ((f32[32,32,8,128]{3,2,1,0:T(8,128)}), f32[32,32,8,128]{3,2,1,0:T(8,128)}, u32[]{:S(2)}, u32[]{:S(2)}) async-start(f32[32,32,8,128]{3,2,1,0:T(8,128)} %get-tuple-element.23), calls=%async_computation.7 | async-start | bytes 8388608 | tf_op jit(solution)/shard_map/all_to_all | solution.py:118
  706.9 98.3 %all-to-all-start.6 = ((f32[32,32,8,128]{3,2,1,0:T(8,128)}), f32[32,32,8,128]{3,2,1,0:T(8,128)}, u32[]{:S(2)}, u32[]{:S(2)}) async-start(f32[32,32,8,128]{3,2,1,0:T(8,128)} %get-tuple-element.22), calls=%async_computation.6 | async-start | bytes 8388608 | tf_op jit(solution)/shard_map/all_to_all | solution.py:118
  912.5 99.0 %copy-start.3 = (f32[32,8,32,128]{3,2,1,0:T(8,128)S(1)}, f32[32,8,32,128]{3,2,1,0:T(8,128)}, u32[]{:S(2)}) copy-start(f32[32,8,32,128]{3,2,1,0:T(8,128)} %get-tuple-element.31) | copy-start | bytes 12582916
  1011.5 97.3 %copy-start.2 = (f32[32,8,32,128]{3,2,1,0:T(8,128)S(1)}, f32[32,8,32,128]{3,2,1,0:T(8,128)}, u32[]{:S(2)}) copy-start(f32[32,8,32,128]{3,2,1,0:T(8,128)} %get-tuple-element.32) | copy-start | bytes 12582916
  1108.8 97.3 %copy-start.1 = (f32[32,8,32,128]{3,2,1,0:T(8,128)S(1)}, f32[32,8,32,128]{3,2,1,0:T(8,128)}, u32[]{:S(2)}) copy-start(f32[32,8,32,128]{3,2,1,0:T(8,128)} %get-tuple-element.33) | copy-start | bytes 12582916
  1206.0 97.3 %copy-start = (f32[32,8,32,128]{3,2,1,0:T(8,128)S(1)}, f32[32,8,32,128]{3,2,1,0:T(8,128)}, u32[]{:S(2)}) copy-start(f32[32,8,32,128]{3,2,1,0:T(8,128)} %get-tuple-element.34) | copy-start | bytes 12582916

commit v2 on v1

--- a/solution.py
+++ b/solution.py
@@ -184,7 +184,7 @@
     )(*fields, *tables)
 
 
-def analysis_kernel(kept, rows_x, narrow, *refs):
+def analysis_kernel(kept, rows_x, narrow, transport, *refs):
     a = [r[0] for r in refs[0:3]]
     u = [r[0] for r in refs[3:6]]
     o = [r[0] for r in refs[6:9]]
@@ -203,42 +203,61 @@
     def to_y(value, table):
         return product(split(value), table_parts(table), PLAIN)
 
+    def pack(value, rows):
+        return jnp.concatenate([value[:rows], value[rows:]], 1)
+
     def store(out, value):
         lanes = value.shape[1] // narrow
+        half, part = rows_x // 2, rows_x // 4
         for w in range(kept // rows_x):
             for n in range(narrow):
-                out[w * narrow + n, 0] = value[w * rows_x : (w + 1) * rows_x, n * lanes : (n + 1) * lanes]
+                owner = 0 if n < narrow // 2 else narrow - 1
+                block = value[w * rows_x : (w + 1) * rows_x]
+                near = block[:, n * lanes : n * lanes + lanes // 2]
+                far = block[:, owner * lanes + lanes // 2 : (owner + 1) * lanes]
+                far = far[(n % 2) * half : (n % 2 + 1) * half]
+                out[w * narrow + n, 0] = jnp.concatenate(
+                    [pack(near[:half], part), pack(near[half:], part), pack(far, part)], 0
+                )
         for d in range(kept // rows_x * narrow, out.shape[0]):
             out[d, 0] = jnp.zeros(out.shape[2:], jnp.float32)
 
+    if transport:
+        for c in range(2):
+            store(outs[c], to_y(modes(cross(u, a, c)), span))
+        return
     tx, ty, tz = [modes(cross(u, a, c)) for c in range(3)]
-    store(outs[3], to_y(tx, span))
-    store(outs[4], to_y(ty, span))
     store(outs[0], to_y(modes(cross(a, o, 0)), span) + to_y(tz, slope))
     store(outs[1], to_y(modes(cross(a, o, 1)) - wave * times_i(tz), span))
     store(outs[2], to_y(modes(cross(a, o, 2)) + wave * times_i(ty), span) - to_y(tx, slope))
 
 
-def analysis(fields, tables, kept, rows_x, wide, narrow):
+def analysis(fields, tables, kept, rows_x, wide, narrow, transport):
     block = fields[0].shape[0]
     owners = wide * narrow
     lanes = 2 * NY // narrow
+    rows = rows_x * 3 // 4
+    count = 2 if transport else 3
     spec = pl.BlockSpec((1, NX, NY), lambda z: (z, 0, 0))
-    out = pl.BlockSpec((owners, 1, rows_x, lanes), lambda z: (0, z, 0, 0))
+    out = pl.BlockSpec((owners, 1, rows, lanes), lambda z: (0, z, 0, 0))
     return pl.pallas_call(
-        functools.partial(analysis_kernel, kept, rows_x, narrow),
+        functools.partial(analysis_kernel, kept, rows_x, narrow, transport),
         grid=(block,),
         in_specs=[spec] * 9 + [whole_spec(t.shape) for t in tables],
-        out_specs=[out] * 5,
-        out_shape=[jax.ShapeDtypeStruct((owners, block, rows_x, lanes), jnp.float32)] * 5,
+        out_specs=[out] * count,
+        out_shape=[jax.ShapeDtypeStruct((owners, block, rows, lanes), jnp.float32)] * count,
         compiler_params=params(),
-        cost_estimate=cost(6.0 * block * 13 * kept * 2 * NX * NY, 4 * 14 * block * NX * NY),
-        name="products_and_analysis",
+        cost_estimate=cost(6.0 * block * 4 * count * kept * 2 * NX * NY, 4 * 12 * block * NX * NY),
+        name="transport_analysis" if transport else "products_and_analysis",
     )(*fields, *tables)
 
 
-def final_kernel(*refs):
-    spectra, adjoint, table, out = refs[:5], refs[5], refs[6], refs[7]
+def final_kernel(narrow, *refs):
+    nears, owns, others = refs[0:5], refs[5:10], refs[10:15]
+    adjoint, table, out = refs[15:]
+    group, side = pl.program_id(0) // 2, pl.program_id(0) % 2
+    lower = lax.axis_index("narrow") < narrow // 2
+    use_own = lower == (group == 0)
     tile, rows_y = adjoint.shape[2], adjoint.shape[3]
     first_x = lax.axis_index("wide") * (tile * pl.num_programs(0)) + pl.program_id(0) * tile
     shape = (rows_y, NZ)
@@ -251,12 +270,24 @@
     kz = number_z.astype(jnp.float32) * (2.0 * math.pi / NZ)
     for row in range(tile):
         parts = []
-        for ref in spectra:
-            flat = ref.reshape(NZ * tile, 2 * rows_y)
-            cells = flat[pl.ds(row, NZ, stride=tile), :].T
+        for near, own, other in zip(nears, owns, others):
+            near, own, other = [
+                r.reshape(NZ * tile, 2 * rows_y)[pl.ds(row, NZ, stride=tile), :] for r in (near, own, other)
+            ]
+            far = jnp.where(use_own, own, other)
+            first, second = jnp.where(lower, near, far), jnp.where(lower, far, near)
+            cells = jnp.where(
+                side == 0,
+                jnp.concatenate([first[:, :rows_y], second[:, :rows_y]], 1),
+                jnp.concatenate([first[:, rows_y:], second[:, rows_y:]], 1),
+            ).T
             both = product(split(cells), table_parts(table), PLAIN)
-            cosine, sine = both[:, :NZ], both[:, NZ:]
-            parts.append((cosine[:rows_y] + sine[rows_y:], cosine[rows_y:] - sine[:rows_y]))
+            quarter = rows_y // 2
+            real, imag = [
+                jnp.concatenate([both[p * quarter : (p + 1) * quarter], both[(p + 2) * quarter : (p + 3) * quarter]], 0)
+                for p in range(2)
+            ]
+            parts.append((real[:, :NZ] + imag[:, NZ:], imag[:, :NZ] - real[:, NZ:]))
         number_x = jnp.full(shape, first_x + row, jnp.int32)
         kx = number_x.astype(jnp.float32) * (2.0 * math.pi / NX)
         ksquare = kx * kx + ky * ky + kz * kz
@@ -272,21 +303,27 @@
                 out[c, part, row] = decay * (adjoint[c, part, row] + keep * (conv[c] - wave * along))
 
 
-def final(spectra, adjoint_hat, table):
+def final(spectra, adjoint_hat, table, narrow):
     rows_x, rows_y = adjoint_hat.shape[2], adjoint_hat.shape[3]
-    tile = min(8, rows_x)
-    spectra = [s.reshape(NZ, rows_x, 2 * rows_y) for s in spectra]
+    tile, lanes = rows_x // 4, 2 * rows_y
+    nears, owns, others = [], [], []
+    for s in spectra:
+        nears.append(s[:, :, : 2 * tile].reshape(NZ, 2, tile, lanes))
+        own = s[:, :, 2 * tile :].reshape(NZ, tile, lanes)
+        owns.append(own)
+        others.append(lax.ppermute(own, "narrow", [(1, 0), (narrow - 2, narrow - 1)]))
     hat = pl.BlockSpec((3, 2, tile, rows_y, NZ), lambda i: (0, 0, i, 0, 0))
+    near = pl.BlockSpec((NZ, 1, tile, lanes), lambda i: (0, i // 2, 0, 0))
     return pl.pallas_call(
-        final_kernel,
-        grid=(rows_x // tile,),
-        in_specs=[pl.BlockSpec((NZ, tile, 2 * rows_y), lambda i: (0, i, 0))] * 5 + [hat, whole_spec(table.shape)],
+        functools.partial(final_kernel, narrow),
+        grid=(4,),
+        in_specs=[near] * 5 + [whole_spec((NZ, tile, lanes))] * 10 + [hat, whole_spec(table.shape)],
         out_specs=hat,
         out_shape=jax.ShapeDtypeStruct(adjoint_hat.shape, jnp.float32),
         compiler_params=params(),
         cost_estimate=cost(30.0 * rows_x * 2 * rows_y * NZ * 2 * NZ, 4 * 22 * rows_x * rows_y * NZ),
         name="depth_analysis_projection",
-    )(*spectra, adjoint_hat, table)
+    )(*nears, *owns, *others, adjoint_hat, table)
 
 
 def local(wide, narrow, adjoint_hat, velocity_hat):
@@ -310,8 +347,11 @@
         return split_table(table.transpose(1, 0, 2, 3, 4).reshape(2 * NY, 2 * NY))
 
     def rows_last(real, imag):
-        table = merged(real, imag).transpose(0, 3, 2, 1).reshape(2, NY, 2, narrow, rows_y)
-        return split_table(table.transpose(0, 1, 3, 2, 4).reshape(2 * NY, 2 * NY))
+        table = merged(real, imag).transpose(0, 3, 2, 1).reshape(2, NY, 2, narrow, 2, rows_y // 2)
+        table = table.transpose(0, 1, 3, 4, 2, 5)
+        upper = table[:, :, narrow // 2 :, ::-1]
+        table = np.concatenate([table[:, :, : narrow // 2], upper], 2)
+        return split_table(table.reshape(2 * NY, 2 * NY))
 
     span = rows_first(cosine, sine)
     slope = rows_first(-wave_y * sine, wave_y * cosine)
@@ -322,20 +362,32 @@
     synth = split_table(np.concatenate([cosine * weights, -sine * weights], 0).T)
     anal = split_table(np.concatenate([cosine[:kept], -sine[:kept]], 0) * scale)
 
-    ux, dzux = [exchange(v) for v in depth(velocity_hat, 0, [depth_table, depth_slope], owners)]
-    uy, dzuy = [exchange(v) for v in depth(velocity_hat, 1, [depth_table, depth_slope], owners)]
-    uz = exchange(depth(velocity_hat, 2, [depth_table], owners)[0])
-    hats = [exchange(depth(adjoint_hat, c, [depth_table], owners)[0]) for c in range(3)]
-    flow = physical_call(
-        velocity_kernel, "velocity_lines", [ux, uy, uz, dzux, dzuy], [span, slope, synth], 6, narrow
-    )
+    buffers = depth(velocity_hat, 2, [depth_table], owners)
+    buffers += depth(velocity_hat, 0, [depth_table, depth_slope], owners)
+    buffers += depth(velocity_hat, 1, [depth_table, depth_slope], owners)
+    for c in range(3):
+        buffers += depth(adjoint_hat, c, [depth_table], owners)
+    arrived = []
+    for place, buffer in enumerate(buffers):
+        if place == 7:
+            uz, ux, dzux, uy, dzuy = arrived[:5]
+            flow = physical_call(
+                velocity_kernel, "velocity_lines", [ux, uy, uz, dzux, dzuy], [span, slope, synth], 6, narrow
+            )
+            buffer, flow = lax.optimization_barrier((buffer, flow))
+        if arrived:
+            buffer, arrived[-1] = lax.optimization_barrier((buffer, arrived[-1]))
+        arrived.append(exchange(buffer))
+    hats = arrived[5:]
     adjoint = [
         physical_call(adjoint_kernel, "adjoint_lines", [hat], [span, synth], 1, narrow)[0] for hat in hats
     ]
-    spectra = analysis(
-        adjoint + list(flow), [anal, back_span, back_slope], kept, rows_x, wide, narrow
-    )
-    return final([exchange(s) for s in spectra], adjoint_hat, final_table)
+    fields, tables = adjoint + list(flow), [anal, back_span, back_slope]
+    transport, curled = [analysis(fields, tables, kept, rows_x, wide, narrow, t) for t in (True, False)]
+    first = exchange(transport[0])
+    second, curled = lax.optimization_barrier((transport[1], curled))
+    spectra = [exchange(s) for s in curled] + [first, exchange(second)]
+    return final(spectra, adjoint_hat, final_table, narrow)
 
 
 def solution(mesh):

time: 1430 us -> 1320 us (0.923)
  blocking collectives: 686 us -> 499 us
  Pallas kernels: 245 us -> 282 us
  local copies, waits for them, and re-layouts: 0.02 us -> 21.6 us
    all_to_all x7 -> x6, blocking collectives: 686 us -> 499 us  [exchange(): return lax.all_to_all(value, axes, split_axis=0, concat_axis=0, tiled=True)]
    pallas_call x2 -> x3, Pallas kernels: 72.6 us -> 109 us  [the longest x2 63.7 us: analysis(): pl.pallas_call(functools.partial(analysis_kernel, kept, rows_x, narrow, t...]
    slice x0 -> x10, local copies, waits for them, and re-layouts: none -> 20.6 us  [the longest x5 11.1 us: final(): nears.append(s[:, :, :2 * tile].reshape(NZ, 2, tile, lanes))]
    all_to_all x6 -> x7, waiting for transfers between devices: 465 us -> 474 us  [exchange(): return lax.all_to_all(value, axes, split_axis=0, concat_axis=0, tiled=True)]
    all_to_all x6 -> x7, starting transfers between devices: 31.5 us -> 35.4 us  [exchange(): return lax.all_to_all(value, axes, split_axis=0, concat_axis=0, tiled=True)]
  transfers between devices with their start and end apart: 6 -> 12, of which waited for: 6 -> 7; matrix products, arithmetic and copies ran while one was open for 0% -> 2% of each run, Pallas kernels for 7% -> 11%
where the time goes in v2:
time: 1320 us
  blocking collectives  499 us (38%)
  waiting for transfers between devices  474 us (36%)
  Pallas kernels  282 us (21%)
  starting transfers between devices  42.1 us (3%)
  local copies, waits for them, and re-layouts  21.6 us (2%)
    all_to_all x6, blocking collectives, exchange(): return lax.all_to_all(value, axes, split_axis=0, concat_axis=0, tiled=True)  499 us
    all_to_all x7, waiting for transfers between devices, exchange(): return lax.all_to_all(value, axes, split_axis=0, concat_axis=0, tiled=True)  474 us
    pallas_call x4, Pallas kernels, physical_call(): pl.pallas_call(functools.partial(kernel, narrow, block), grid=(block,), i...  101 us
    pallas_call x6, Pallas kernels, depth(): pl.pallas_call(functools.partial(depth_kernel, count, by_owner), grid=(ro...  71.9 us
    pallas_call x2, Pallas kernels, analysis(): pl.pallas_call(functools.partial(analysis_kernel, kept, rows_x, narrow, t...  63.7 us
    pallas_call x1, Pallas kernels, final(): pl.pallas_call(functools.partial(final_kernel, narrow), grid=(4,), in_spe...  45.7 us
    all_to_all x7, starting transfers between devices, exchange(): return lax.all_to_all(value, axes, split_axis=0, concat_axis=0, tiled=True)  35.4 us
  transfers between devices with their start and end apart: 12, of which 7 were waited for; matrix products, arithmetic and copies ran while one was open for 2% of the time, Pallas kernels for 11%

profile of v2, /device:TPU:0, one launch (start us, length us, event | category | flops | bytes accessed | tf_op | source)
XLA Modules:
  0.0 1319.0 jit_solution(4454471734031884027)
XLA Ops:
  0.0 9.7 depth_synthesis.10
  17.1 16.6 %depth_synthesis.9 = (f32[32,32,8,128]{3,2,1,0:T(8,128)}, f32[32,32,8,128]{3,2,1,0:T(8,128)}) custom-call(f32[3,2,32,64,256]{4,3,2,1,0:T(8,128)} %field_ref.10, bf16[2,256,512]{2,1,0:T(8,128)(2,1)} %constant.16.clone.refs_0_.refs_16_, bf16[2,256,512]{2,1,0:T(8,128)(2,1)} %constant.17.clone.refs_1_), custom_call_target="tpu_custom_call" | custom-call | flops 6442450944 | bytes 12582912 | tf_op jit(solution)/shard_map/depth_synthesis/pallas_call | solution.py:101
  33.7 77.7 %all-to-all-done = f32[32,32,8,128]{3,2,1,0:T(8,128)} async-done(((f32[32,32,8,128]{3,2,1,0:T(8,128)}), f32[32,32,8,128]{3,2,1,0:T(8,128)}, u32[]{:S(2)}, u32[]{:S(2)}) %all-to-all-start) | async-done | bytes 4194336 | tf_op jit(solution)/shard_map/all_to_all | solution.py:118
  111.5 99.0 %all_to_all.65 = f32[32,32,8,128]{3,2,1,0:T(8,128)} all-to-all(f32[32,32,8,128]{3,2,1,0:T(8,128)} %get-tuple-element.49), channel_id=1, replica_groups=mesh['narrow'=4,'wide'=8] {'wide','narrow'}, dimensions={0} | all-to-all | bytes 8388608 | tf_op jit(solution)/shard_map/all_to_all | solution.py:118
  214.4 16.7 %depth_synthesis.8 = (f32[32,32,8,128]{3,2,1,0:T(8,128)}, f32[32,32,8,128]{3,2,1,0:T(8,128)}) custom-call(f32[3,2,32,64,256]{4,3,2,1,0:T(8,128)} %field_ref.10, bf16[2,256,512]{2,1,0:T(8,128)(2,1)} %constant.16.clone.refs_0_.refs_16_, bf16[2,256,512]{2,1,0:T(8,128)(2,1)} %constant.17.clone.refs_1_), custom_call_target="tpu_custom_call" | custom-call | flops 6442450944 | bytes 12582912 | tf_op jit(solution)/shard_map/depth_synthesis/pallas_call | solution.py:101
  231.0 77.7 %all-to-all-done.2 = f32[32,32,8,128]{3,2,1,0:T(8,128)} async-done(((f32[32,32,8,128]{3,2,1,0:T(8,128)}), f32[32,32,8,128]{3,2,1,0:T(8,128)}, u32[]{:S(2)}, u32[]{:S(2)}) %all-to-all-start.2) | async-done | bytes 4194336 | tf_op jit(solution)/shard_map/all_to_all | solution.py:118
  308.7 99.0 %all_to_all.66 = f32[32,32,8,128]{3,2,1,0:T(8,128)} all-to-all(f32[32,32,8,128]{3,2,1,0:T(8,128)} %get-tuple-element.51), channel_id=1, replica_groups=mesh['narrow'=4,'wide'=8] {'wide','narrow'}, dimensions={0} | all-to-all | bytes 8388608 | tf_op jit(solution)/shard_map/all_to_all | solution.py:118
  421.2 84.8 %all-to-all-done.4 = f32[32,32,8,128]{3,2,1,0:T(8,128)} async-done(((f32[32,32,8,128]{3,2,1,0:T(8,128)}), f32[32,32,8,128]{3,2,1,0:T(8,128)}, u32[]{:S(2)}, u32[]{:S(2)}) %all-to-all-start.4) | async-done | bytes 4194336 | tf_op jit(solution)/shard_map/all_to_all | solution.py:118
  511.4 9.7 depth_synthesis.6
  521.0 84.7 %all-to-all-done.5 = f32[32,32,8,128]{3,2,1,0:T(8,128)} async-done(((f32[32,32,8,128]{3,2,1,0:T(8,128)}), f32[32,32,8,128]{3,2,1,0:T(8,128)}, u32[]{:S(2)}, u32[]{:S(2)}) %all-to-all-start.5) | async-done | bytes 4194336 | tf_op jit(solution)/shard_map/all_to_all | solution.py:118
  621.0 62.3 %velocity_lines.1 = (f32[8,512,256]{2,1,0:T(8,128)}, f32[8,512,256]{2,1,0:T(8,128)}, f32[8,512,256]{2,1,0:T(8,128)}, f32[8,512,256]{2,1,0:T(8,128)}, f32[8,512,256]{2,1,0:T(8,128)}, /*index=5*/f32[8,512,256]{2,1,0:T(8,128)}) custom-call(f32[32,256,128]{2,1,0:T(8,128)} %bitcast.18, f32[32,256,128]{2,1,0:T(8,128)} %bitcast.19, ...), custom_call_target="tpu_custom_call" | custom-call | flops 38654705664 | bytes 50331648 | tf_op jit(solution)/shard_map/velocity_lines/pallas_call | solution.py:175
  683.3 22.3 %all-to-all-done.6 = f32[32,32,8,128]{3,2,1,0:T(8,128)} async-done(((f32[32,32,8,128]{3,2,1,0:T(8,128)}), f32[32,32,8,128]{3,2,1,0:T(8,128)}, u32[]{:S(2)}, u32[]{:S(2)}) %all-to-all-start.6) | async-done | bytes 4194336 | tf_op jit(solution)/shard_map/all_to_all | solution.py:118
  711.1 13.0 adjoint_lines.3.refs_0_
  724.1 12.9 adjoint_lines.4.refs_1_
  737.0 68.4 %all-to-all-done.7 = f32[32,32,8,128]{3,2,1,0:T(8,128)} async-done(((f32[32,32,8,128]{3,2,1,0:T(8,128)}), f32[32,32,8,128]{3,2,1,0:T(8,128)}, u32[]{:S(2)}, u32[]{:S(2)}) %all-to-all-start.7) | async-done | bytes 4194336 | tf_op jit(solution)/shard_map/all_to_all | solution.py:118
  805.3 12.9 adjoint_lines.5.refs_2_
  818.3 40.4 %products_and_analysis.1 = (f32[32,8,24,128]{3,2,1,0:T(8,128)}, f32[32,8,24,128]{3,2,1,0:T(8,128)}, f32[32,8,24,128]{3,2,1,0:T(8,128)}) custom-call(f32[8,512,256]{2,1,0:T(8,128)} %adjoint_lines.3.refs_0_, f32[8,512,256]{2,1,0:T(8,128)} %adjoint_lines.4.refs_1_, f32[8,512,256]{2,1,0:T(8,128)} %adjoint_lines.5.refs_2_, ...), custom_call_target="tpu_custom_call" | custom-call | flops 28991029248 | bytes 50331648 | tf_op jit(solution)/shard_map/products_and_analysis/pallas_call | solution.py:243
  858.7 23.3 %transport_analysis.1 = (f32[32,8,24,128]{3,2,1,0:T(8,128)}, f32[32,8,24,128]{3,2,1,0:T(8,128)}) custom-call(f32[8,512,256]{2,1,0:T(8,128)} %adjoint_lines.3.refs_0_, f32[8,512,256]{2,1,0:T(8,128)} %adjoint_lines.4.refs_1_, f32[8,512,256]{2,1,0:T(8,128)} %adjoint_lines.5.refs_2_, f32[8,512,256]{2,1,0:T(8,128)} %get-tuple-element.70.refs_3_, ...), custom_call_target="tpu_custom_call" | custom-call | flops 19327352832 | bytes 50331648 | tf_op jit(solution)/shard_map/transport_analysis/pallas_call | solution.py:243
  882.0 76.4 %all_to_all.67 = f32[32,8,24,128]{3,2,1,0:T(8,128)S(1)} all-to-all(f32[32,8,24,128]{3,2,1,0:T(8,128)} %get-tuple-element.80), channel_id=1, replica_groups=mesh['narrow'=4,'wide'=8] {'wide','narrow'}, dimensions={0} | all-to-all | bytes 6291456 | tf_op jit(solution)/shard_map/all_to_all | solution.py:118
  958.4 74.7 %all_to_all.68 = f32[32,8,24,128]{3,2,1,0:T(8,128)} all-to-all(f32[32,8,24,128]{3,2,1,0:T(8,128)S(1)} %copy-done.4), channel_id=1, replica_groups=mesh['narrow'=4,'wide'=8] {'wide','narrow'}, dimensions={0} | all-to-all | bytes 6291456 | tf_op jit(solution)/shard_map/all_to_all | solution.py:118
  1033.2 74.7 %all_to_all.69 = f32[32,8,24,128]{3,2,1,0:T(8,128)} all-to-all(f32[32,8,24,128]{3,2,1,0:T(8,128)S(1)} %copy-done.3), channel_id=1, replica_groups=mesh['narrow'=4,'wide'=8] {'wide','narrow'}, dimensions={0} | all-to-all | bytes 6291456 | tf_op jit(solution)/shard_map/all_to_all | solution.py:118
  1107.9 74.7 %all_to_all.70 = f32[32,8,24,128]{3,2,1,0:T(8,128)} all-to-all(f32[32,8,24,128]{3,2,1,0:T(8,128)S(1)} %copy-done.2), channel_id=1, replica_groups=mesh['narrow'=4,'wide'=8] {'wide','narrow'}, dimensions={0} | all-to-all | bytes 6291456 | tf_op jit(solution)/shard_map/all_to_all | solution.py:118
  1199.7 58.5 %all-to-all-done.11 = f32[32,8,24,128]{3,2,1,0:T(8,128)} async-done(((f32[32,8,24,128]{3,2,1,0:T(8,128)}), f32[32,8,24,128]{3,2,1,0:T(8,128)}, u32[]{:S(2)}, u32[]{:S(2)}) %all-to-all-start.11) | async-done | bytes 3145760 | tf_op jit(solution)/shard_map/all_to_all | solution.py:118
  1273.3 45.7 %depth_analysis_projection.1 = f32[3,2,32,64,256]{4,3,2,1,0:T(8,128)} custom-call(f32[256,2,8,128]{3,2,1,0:T(8,128)} %bitcast.22, f32[256,2,8,128]{3,2,1,0:T(8,128)} %bitcast.23, f32[256,2,8,128]{3,2,1,0:T(8,128)} %bitcast.20, f32[256,2,8,128]{3,2,1,0:T(8,128)} %bitcast.24, f32[256,2,8,128]{3,2,1,0:T(8,128)} %bitcast.21, f32[256,8,128]{2,1,0:T(8,128)} %bitcast.13.refs_5_, ...), custom_call_target="tpu_custom_call" | custom-call | flops 16106127360 | bytes 46137344 | tf_op jit(solution)/shard_map/depth_analysis_projection/pallas_call | solution.py:317
  (43 shorter events, 82.9 us)
Async XLA Ops:
  9.7 101.8 %all-to-all-start = ((f32[32,32,8,128]{3,2,1,0:T(8,128)}), f32[32,32,8,128]{3,2,1,0:T(8,128)}, u32[]{:S(2)}, u32[]{:S(2)}) async-start(f32[32,32,8,128]{3,2,1,0:T(8,128)} %depth_synthesis.10), calls=%async_computation | async-start | bytes 8388608 | tf_op jit(solution)/shard_map/all_to_all | solution.py:118
  210.5 98.2 %all-to-all-start.2 = ((f32[32,32,8,128]{3,2,1,0:T(8,128)}), f32[32,32,8,128]{3,2,1,0:T(8,128)}, u32[]{:S(2)}, u32[]{:S(2)}) async-start(f32[32,32,8,128]{3,2,1,0:T(8,128)} %get-tuple-element.50), calls=%async_computation.2 | async-start | bytes 8388608 | tf_op jit(solution)/shard_map/all_to_all | solution.py:118
  407.7 98.2 %all-to-all-start.4 = ((f32[32,32,8,128]{3,2,1,0:T(8,128)}), f32[32,32,8,128]{3,2,1,0:T(8,128)}, u32[]{:S(2)}, u32[]{:S(2)}) async-start(f32[32,32,8,128]{3,2,1,0:T(8,128)} %get-tuple-element.52), calls=%async_computation.4 | async-start | bytes 8388608 | tf_op jit(solution)/shard_map/all_to_all | solution.py:118
  506.0 99.8 %all-to-all-start.5 = ((f32[32,32,8,128]{3,2,1,0:T(8,128)}), f32[32,32,8,128]{3,2,1,0:T(8,128)}, u32[]{:S(2)}, u32[]{:S(2)}) async-start(f32[32,32,8,128]{3,2,1,0:T(8,128)} %depth_synthesis.7), calls=%async_computation.5 | async-start | bytes 8388608 | tf_op jit(solution)/shard_map/all_to_all | solution.py:118
  605.7 99.8 %all-to-all-start.6 = ((f32[32,32,8,128]{3,2,1,0:T(8,128)}), f32[32,32,8,128]{3,2,1,0:T(8,128)}, u32[]{:S(2)}, u32[]{:S(2)}) async-start(f32[32,32,8,128]{3,2,1,0:T(8,128)} %depth_synthesis.6), calls=%async_computation.6 | async-start | bytes 8388608 | tf_op jit(solution)/shard_map/all_to_all | solution.py:118
  705.6 99.8 %all-to-all-start.7 = ((f32[32,32,8,128]{3,2,1,0:T(8,128)}), f32[32,32,8,128]{3,2,1,0:T(8,128)}, u32[]{:S(2)}, u32[]{:S(2)}) async-start(f32[32,32,8,128]{3,2,1,0:T(8,128)} %depth_synthesis.11), calls=%async_computation.7 | async-start | bytes 8388608 | tf_op jit(solution)/shard_map/all_to_all | solution.py:118
  882.0 76.4 %copy-start.4 = (f32[32,8,24,128]{3,2,1,0:T(8,128)S(1)}, f32[32,8,24,128]{3,2,1,0:T(8,128)}, u32[]{:S(2)}) copy-start(f32[32,8,24,128]{3,2,1,0:T(8,128)} %get-tuple-element.81) | copy-start | bytes 9437188
  958.4 74.8 %copy-start.3 = (f32[32,8,24,128]{3,2,1,0:T(8,128)S(1)}, f32[32,8,24,128]{3,2,1,0:T(8,128)}, u32[]{:S(2)}) copy-start(f32[32,8,24,128]{3,2,1,0:T(8,128)} %get-tuple-element.82) | copy-start | bytes 9437188
  1033.2 74.8 %copy-start.2 = (f32[32,8,24,128]{3,2,1,0:T(8,128)S(1)}, f32[32,8,24,128]{3,2,1,0:T(8,128)}, u32[]{:S(2)}) copy-start(f32[32,8,24,128]{3,2,1,0:T(8,128)} %get-tuple-element.84) | copy-start | bytes 9437188
  1182.7 75.5 %all-to-all-start.11 = ((f32[32,8,24,128]{3,2,1,0:T(8,128)}), f32[32,8,24,128]{3,2,1,0:T(8,128)}, u32[]{:S(2)}, u32[]{:S(2)}) async-start(f32[32,8,24,128]{3,2,1,0:T(8,128)} %get-tuple-element.83), calls=%async_computation.11 | async-start | bytes 6291456 | tf_op jit(solution)/shard_map/all_to_all | solution.py:118
  1187.6 84.7 %collective-permute-start = (f32[256,8,128]{2,1,0:T(8,128)}, f32[256,8,128]{2,1,0:T(8,128)}, u32[]{:S(2)}, u32[]{:S(2)}) collective-permute-start(f32[256,8,128]{2,1,0:T(8,128)} %bitcast.13.refs_5_), channel_id=1, source_target_pairs={{8,0},{16,24},{9,1},{17,25},{10,2},{18,26},{11,3},{19,27},{12,4},{... | collective-permute-start | bytes 3145736 | tf_op jit(solution)/shard_map/ppermute | solution.py:314
  1191.2 81.1 %collective-permute-start.1 = (f32[256,8,128]{2,1,0:T(8,128)}, f32[256,8,128]{2,1,0:T(8,128)}, u32[]{:S(2)}, u32[]{:S(2)}) collective-permute-start(f32[256,8,128]{2,1,0:T(8,128)} %bitcast.14.refs_6_), channel_id=1, source_target_pairs={{8,0},{16,24},{9,1},{17,25},{10,2},{18,26},{11,3},{19,27},{12,4},{... | collective-permute-start | bytes 3145736 | tf_op jit(solution)/shard_map/ppermute | solution.py:314
  1194.8 77.5 %collective-permute-start.2 = (f32[256,8,128]{2,1,0:T(8,128)}, f32[256,8,128]{2,1,0:T(8,128)}, u32[]{:S(2)}, u32[]{:S(2)}) collective-permute-start(f32[256,8,128]{2,1,0:T(8,128)} %bitcast.15.refs_7_), channel_id=1, source_target_pairs={{8,0},{16,24},{9,1},{17,25},{10,2},{18,26},{11,3},{19,27},{12,4},{... | collective-permute-start | bytes 3145736 | tf_op jit(solution)/shard_map/ppermute | solution.py:314
  1198.4 73.9 %collective-permute-start.4 = (f32[256,8,128]{2,1,0:T(8,128)}, f32[256,8,128]{2,1,0:T(8,128)}, u32[]{:S(2)}, u32[]{:S(2)}) collective-permute-start(f32[256,8,128]{2,1,0:T(8,128)} %bitcast.17.refs_9_), channel_id=1, source_target_pairs={{8,0},{16,24},{9,1},{17,25},{10,2},{18,26},{11,3},{19,27},{12,4},{... | collective-permute-start | bytes 3145736 | tf_op jit(solution)/shard_map/ppermute | solution.py:314
  1258.2 6.2 copy-start.1
  1259.6 6.3 copy-start.5
  1259.6 12.7 collective-permute-start.3
  1264.4 3.2 copy-start
  1272.3 1.0 copy-start.6

commit v3 on v2

--- a/solution.py
+++ b/solution.py
@@ -138,7 +138,7 @@
     return product(table_parts(synth), split(stacked(value)), PLAIN)
 
 
-def velocity_kernel(narrow, block, *refs):
+def vorticity_kernel(narrow, block, *refs):
     ux, uy, uz, dzux, dzuy, span, slope, synth = refs[:8]
     outs = refs[8:]
     plane = pl.program_id(0)
@@ -150,20 +150,14 @@
     def to_y(value, table):
         return product(value, table_parts(table), PLAIN)
 
-    rows_x = rows(ux)
-    value_x = to_y(rows_x, span)
-    outs[0][0] = lines(value_x, synth)
-    value_y = to_y(rows(uy), span)
-    outs[1][0] = lines(value_y, synth)
-    rows_z = rows(uz)
-    value_z = to_y(rows_z, span)
-    outs[2][0] = lines(value_z, synth)
-    outs[3][0] = lines(to_y(rows_z, slope) - to_y(rows(dzuy), span), synth)
-    outs[4][0] = lines(to_y(rows(dzux), span) - wave * times_i(value_z), synth)
-    outs[5][0] = lines(wave * times_i(value_y) - to_y(rows_x, slope), synth)
-
-
-def adjoint_kernel(narrow, block, field, span, synth, out):
+    rows_x, rows_z = rows(ux), rows(uz)
+    value_y, value_z = to_y(rows(uy), span), to_y(rows_z, span)
+    outs[0][0] = lines(to_y(rows_z, slope) - to_y(rows(dzuy), span), synth)
+    outs[1][0] = lines(to_y(rows(dzux), span) - wave * times_i(value_z), synth)
+    outs[2][0] = lines(wave * times_i(value_y) - to_y(rows_x, slope), synth)
+
+
+def field_kernel(narrow, block, field, span, synth, out):
     rows = plane_rows(field, narrow, block, pl.program_id(0))
     out[0] = lines(product(rows, table_parts(span), PLAIN), synth)
 
@@ -187,9 +181,9 @@
 def analysis_kernel(kept, rows_x, narrow, transport, *refs):
     a = [r[0] for r in refs[0:3]]
     u = [r[0] for r in refs[3:6]]
-    o = [r[0] for r in refs[6:9]]
-    anal, span, slope = refs[9:12]
-    outs = refs[12:]
+    o = [] if transport else [r[0] for r in refs[6:9]]
+    anal, span, slope = refs[6 + len(o) : 9 + len(o)]
+    outs = refs[9 + len(o) :]
     wave = lax.broadcasted_iota(jnp.int32, (kept, 2 * NY), 0).astype(jnp.float32) * (2.0 * math.pi / NX)
 
     def cross(p, q, c):
@@ -243,7 +237,7 @@
     return pl.pallas_call(
         functools.partial(analysis_kernel, kept, rows_x, narrow, transport),
         grid=(block,),
-        in_specs=[spec] * 9 + [whole_spec(t.shape) for t in tables],
+        in_specs=[spec] * len(fields) + [whole_spec(t.shape) for t in tables],
         out_specs=[out] * count,
         out_shape=[jax.ShapeDtypeStruct((owners, block, rows, lanes), jnp.float32)] * count,
         compiler_params=params(),
@@ -255,11 +249,12 @@
 def final_kernel(narrow, *refs):
     nears, owns, others = refs[0:5], refs[5:10], refs[10:15]
     adjoint, table, out = refs[15:]
-    group, side = pl.program_id(0) // 2, pl.program_id(0) % 2
+    count, rows_y = adjoint.shape[4], adjoint.shape[5]
+    tile, lanes = nears[0].shape[2], nears[0].shape[3]
+    group, step = pl.program_id(0), pl.program_id(1)
     lower = lax.axis_index("narrow") < narrow // 2
     use_own = lower == (group == 0)
-    tile, rows_y = adjoint.shape[2], adjoint.shape[3]
-    first_x = lax.axis_index("wide") * (tile * pl.num_programs(0)) + pl.program_id(0) * tile
+    first_x = lax.axis_index("wide") * (4 * tile) + group * 2 * tile + step * count
     shape = (rows_y, NZ)
     number_y = lax.broadcasted_iota(jnp.int32, shape, 0) + lax.axis_index("narrow") * rows_y
     number_y = jnp.where(number_y < NY // 2, number_y, number_y - NY)
@@ -268,62 +263,64 @@
     keep_yz = (3 * jnp.abs(number_y) < NY) & (3 * jnp.abs(number_z) < NZ)
     ky = number_y.astype(jnp.float32) * (2.0 * math.pi / NY)
     kz = number_z.astype(jnp.float32) * (2.0 * math.pi / NZ)
-    for row in range(tile):
-        parts = []
-        for near, own, other in zip(nears, owns, others):
+    quarter = rows_y // 2
+
+    def modes(ref_values):
+        return product(split(ref_values.T), table_parts(table), PLAIN)
+
+    for row in range(count):
+        pairs = []
+        for refs_of in zip(nears, owns, others):
             near, own, other = [
-                r.reshape(NZ * tile, 2 * rows_y)[pl.ds(row, NZ, stride=tile), :] for r in (near, own, other)
+                r.reshape(NZ * tile, lanes)[pl.ds(step * count + row, NZ, stride=tile), :] for r in refs_of
             ]
             far = jnp.where(use_own, own, other)
-            first, second = jnp.where(lower, near, far), jnp.where(lower, far, near)
-            cells = jnp.where(
-                side == 0,
-                jnp.concatenate([first[:, :rows_y], second[:, :rows_y]], 1),
-                jnp.concatenate([first[:, rows_y:], second[:, rows_y:]], 1),
-            ).T
-            both = product(split(cells), table_parts(table), PLAIN)
-            quarter = rows_y // 2
-            real, imag = [
-                jnp.concatenate([both[p * quarter : (p + 1) * quarter], both[(p + 2) * quarter : (p + 3) * quarter]], 0)
-                for p in range(2)
-            ]
-            parts.append((real[:, :NZ] + imag[:, NZ:], imag[:, :NZ] - real[:, NZ:]))
-        number_x = jnp.full(shape, first_x + row, jnp.int32)
-        kx = number_x.astype(jnp.float32) * (2.0 * math.pi / NX)
-        ksquare = kx * kx + ky * ky + kz * kz
-        inverse = 1.0 / (ksquare + (ksquare == 0).astype(jnp.float32))
-        keep = (keep_yz & (3 * number_x < NX)).astype(jnp.float32) * section_step
-        decay = jnp.exp(-viscous_rate * ksquare)
-        a1, a2, a3, t1, t2 = parts
-        real = (a1[0] + kz * t2[1], a2[0] - kz * t1[1], a3[0])
-        imag = (a1[1] - kz * t2[0], a2[1] + kz * t1[0], a3[1])
-        for part, conv in enumerate((real, imag)):
-            along = (kx * conv[0] + ky * conv[1] + kz * conv[2]) * inverse
-            for c, wave in enumerate((kx, ky, kz)):
-                out[c, part, row] = decay * (adjoint[c, part, row] + keep * (conv[c] - wave * along))
+            pairs.append((modes(jnp.where(lower, near, far)), modes(jnp.where(lower, far, near))))
+        for side in range(2):
+            parts = []
+            for first, second in pairs:
+                real, imag = [
+                    jnp.concatenate([v[at : at + quarter] for v in (first, second)], 0)
+                    for at in (side * rows_y, side * rows_y + quarter)
+                ]
+                parts.append((real[:, :NZ] + imag[:, NZ:], imag[:, :NZ] - real[:, NZ:]))
+            number_x = jnp.full(shape, first_x + side * tile + row, jnp.int32)
+            kx = number_x.astype(jnp.float32) * (2.0 * math.pi / NX)
+            ksquare = kx * kx + ky * ky + kz * kz
+            inverse = 1.0 / (ksquare + (ksquare == 0).astype(jnp.float32))
+            keep = (keep_yz & (3 * number_x < NX)).astype(jnp.float32) * section_step
+            decay = jnp.exp(-viscous_rate * ksquare)
+            a1, a2, a3, t1, t2 = parts
+            real = (a1[0] + kz * t2[1], a2[0] - kz * t1[1], a3[0])
+            imag = (a1[1] - kz * t2[0], a2[1] + kz * t1[0], a3[1])
+            for part, conv in enumerate((real, imag)):
+                along = (kx * conv[0] + ky * conv[1] + kz * conv[2]) * inverse
+                for c, wave in enumerate((kx, ky, kz)):
+                    old = adjoint[c, part, 0, side, row]
+                    out[c, part, 0, side, row] = decay * (old + keep * (conv[c] - wave * along))
 
 
 def final(spectra, adjoint_hat, table, narrow):
     rows_x, rows_y = adjoint_hat.shape[2], adjoint_hat.shape[3]
     tile, lanes = rows_x // 4, 2 * rows_y
-    nears, owns, others = [], [], []
-    for s in spectra:
-        nears.append(s[:, :, : 2 * tile].reshape(NZ, 2, tile, lanes))
-        own = s[:, :, 2 * tile :].reshape(NZ, tile, lanes)
-        owns.append(own)
-        others.append(lax.ppermute(own, "narrow", [(1, 0), (narrow - 2, narrow - 1)]))
-    hat = pl.BlockSpec((3, 2, tile, rows_y, NZ), lambda i: (0, 0, i, 0, 0))
-    near = pl.BlockSpec((NZ, 1, tile, lanes), lambda i: (0, i // 2, 0, 0))
-    return pl.pallas_call(
+    count = min(2, tile)
+    spectra = [s.reshape(NZ, 3, tile, lanes) for s in spectra]
+    others = [lax.ppermute(s[:, 2], "narrow", [(1, 0), (narrow - 2, narrow - 1)]) for s in spectra]
+    paired = (3, 2, 2, 2, tile, rows_y, NZ)
+    hat = pl.BlockSpec((3, 2, 1, 2, count, rows_y, NZ), lambda g, i: (0, 0, g, 0, i, 0, 0))
+    near = pl.BlockSpec((NZ, 1, tile, lanes), lambda g, i: (0, g, 0, 0))
+    own = pl.BlockSpec((NZ, 1, tile, lanes), lambda g, i: (0, 2, 0, 0), pipeline_mode=pl.Buffered(1))
+    result = pl.pallas_call(
         functools.partial(final_kernel, narrow),
-        grid=(4,),
-        in_specs=[near] * 5 + [whole_spec((NZ, tile, lanes))] * 10 + [hat, whole_spec(table.shape)],
+        grid=(2, tile // count),
+        in_specs=[near] * 5 + [own] * 5 + [whole_spec((NZ, tile, lanes))] * 5 + [hat, whole_spec(table.shape)],
         out_specs=hat,
-        out_shape=jax.ShapeDtypeStruct(adjoint_hat.shape, jnp.float32),
+        out_shape=jax.ShapeDtypeStruct(paired, jnp.float32),
         compiler_params=params(),
         cost_estimate=cost(30.0 * rows_x * 2 * rows_y * NZ * 2 * NZ, 4 * 22 * rows_x * rows_y * NZ),
         name="depth_analysis_projection",
-    )(*nears, *owns, *others, adjoint_hat, table)
+    )(*spectra, *spectra, *others, adjoint_hat.reshape(paired), table)
+    return result.reshape(adjoint_hat.shape)
 
 
 def local(wide, narrow, adjoint_hat, velocity_hat):
@@ -362,31 +359,43 @@
     synth = split_table(np.concatenate([cosine * weights, -sine * weights], 0).T)
     anal = split_table(np.concatenate([cosine[:kept], -sine[:kept]], 0) * scale)
 
-    buffers = depth(velocity_hat, 2, [depth_table], owners)
-    buffers += depth(velocity_hat, 0, [depth_table, depth_slope], owners)
-    buffers += depth(velocity_hat, 1, [depth_table, depth_slope], owners)
-    for c in range(3):
-        buffers += depth(adjoint_hat, c, [depth_table], owners)
-    arrived = []
-    for place, buffer in enumerate(buffers):
-        if place == 7:
-            uz, ux, dzux, uy, dzuy = arrived[:5]
-            flow = physical_call(
-                velocity_kernel, "velocity_lines", [ux, uy, uz, dzux, dzuy], [span, slope, synth], 6, narrow
-            )
-            buffer, flow = lax.optimization_barrier((buffer, flow))
+    (bz,) = depth(velocity_hat, 2, [depth_table], owners)
+    bx, dx = depth(velocity_hat, 0, [depth_table, depth_slope], owners)
+    by, dy = depth(velocity_hat, 1, [depth_table, depth_slope], owners)
+    buffers = [bz, bx, by] + [depth(adjoint_hat, c, [depth_table], owners)[0] for c in range(3)]
+
+    def tie(*values):
+        return lax.optimization_barrier(values)
+
+    def field_lines(value):
+        return physical_call(field_kernel, "field_lines", [value], [span, synth], 1, narrow)[0]
+
+    arrived, cells = [], []
+    for buffer in buffers:
+        if len(arrived) >= 2:
+            cells.append(field_lines(arrived[-2]))
+            buffer, cells[-1] = tie(buffer, cells[-1])
         if arrived:
-            buffer, arrived[-1] = lax.optimization_barrier((buffer, arrived[-1]))
+            buffer, arrived[-1] = tie(buffer, arrived[-1])
         arrived.append(exchange(buffer))
-    hats = arrived[5:]
-    adjoint = [
-        physical_call(adjoint_kernel, "adjoint_lines", [hat], [span, synth], 1, narrow)[0] for hat in hats
-    ]
-    fields, tables = adjoint + list(flow), [anal, back_span, back_slope]
-    transport, curled = [analysis(fields, tables, kept, rows_x, wide, narrow, t) for t in (True, False)]
-    first = exchange(transport[0])
-    second, curled = lax.optimization_barrier((transport[1], curled))
-    spectra = [exchange(s) for s in curled] + [first, exchange(second)]
+    dx, arrived[5], last = tie(dx, arrived[5], field_lines(arrived[4]))
+    cells.append(last)
+    dzux = exchange(dx)
+    cells.append(field_lines(arrived[5]))
+    fields = cells[3:6] + [cells[1], cells[2], cells[0]]
+    tables = [anal, back_span, back_slope]
+    transport = analysis(fields, tables, kept, rows_x, wide, narrow, True)
+    dy, dzux, first, second = tie(dy, dzux, *transport)
+    dzuy = exchange(dy)
+    first, dzuy = tie(first, dzuy)
+    first = exchange(first)
+    flow = [arrived[1], arrived[2], arrived[0], dzux, dzuy]
+    curl = physical_call(vorticity_kernel, "vorticity_lines", flow, [span, slope, synth], 3, narrow)
+    second, first, *curl = tie(second, first, *curl)
+    second = exchange(second)
+    curled = analysis(fields + list(curl), tables, kept, rows_x, wide, narrow, False)
+    second, *curled = tie(second, *curled)
+    spectra = [exchange(c) for c in curled] + [first, second]
     return final(spectra, adjoint_hat, final_table, narrow)
 
 

time: 1320 us -> 1230 us (0.932)
  blocking collectives: 499 us -> 250 us
  waiting for transfers between devices: 474 us -> 620 us
  starting transfers between devices: 42.1 us -> 58.7 us
    all_to_all x6 -> x3, blocking collectives: 499 us -> 250 us  [exchange(): return lax.all_to_all(value, axes, split_axis=0, concat_axis=0, tiled=True)]
    all_to_all x7 -> x10, waiting for transfers between devices: 474 us -> 616 us  [exchange(): return lax.all_to_all(value, axes, split_axis=0, concat_axis=0, tiled=True)]
    pallas_call x4 -> x7, Pallas kernels: 101 us -> 125 us  [physical_call(): pl.pallas_call(functools.partial(kernel, narrow, block), grid=(block,), i...]
    slice x10 -> x0, local copies, waits for them, and re-layouts: 20.6 us -> none  [the longest x5 11.1 us: final(): nears.append(s[:, :, :2 * tile].reshape(NZ, 2, tile, lanes))]
    all_to_all x7 -> x10, starting transfers between devices: 35.4 us -> 52.3 us  [exchange(): return lax.all_to_all(value, axes, split_axis=0, concat_axis=0, tiled=True)]
  transfers between devices with their start and end apart: 12 -> 15, of which waited for: 7 -> 13; matrix products, arithmetic and copies ran while one was open for 2% -> 1% of each run, Pallas kernels for 11% -> 20%
where the time goes in v3:
time: 1230 us
  waiting for transfers between devices  620 us (50%)
  Pallas kernels  292 us (24%)
  blocking collectives  250 us (20%)
  starting transfers between devices  58.7 us (5%)
    all_to_all x10, waiting for transfers between devices, exchange(): return lax.all_to_all(value, axes, split_axis=0, concat_axis=0, tiled=True)  616 us
    all_to_all x3, blocking collectives, exchange(): return lax.all_to_all(value, axes, split_axis=0, concat_axis=0, tiled=True)  250 us
    pallas_call x7, Pallas kernels, physical_call(): pl.pallas_call(functools.partial(kernel, narrow, block), grid=(block,), i...  125 us
    pallas_call x6, Pallas kernels, depth(): pl.pallas_call(functools.partial(depth_kernel, count, by_owner), grid=(ro...  71.9 us
    pallas_call x2, Pallas kernels, analysis(): pl.pallas_call(functools.partial(analysis_kernel, kept, rows_x, narrow, t...  61.6 us
    all_to_all x10, starting transfers between devices, exchange(): return lax.all_to_all(value, axes, split_axis=0, concat_axis=0, tiled=True)  52.3 us
    pallas_call x1, Pallas kernels, final(): pl.pallas_call(functools.partial(final_kernel, narrow), grid=(2, tile //...  32.6 us
  transfers between devices with their start and end apart: 15, of which 13 were waited for; matrix products, arithmetic and copies ran while one was open for 1% of the time, Pallas kernels for 20%

profile of v3, /device:TPU:0, one launch (start us, length us, event | category | flops | bytes accessed | tf_op | source)
XLA Modules:
  0.0 1229.4 jit_solution(14997899135203746843)
XLA Ops:
  17.0 16.7 %depth_synthesis.7 = (f32[32,32,8,128]{3,2,1,0:T(8,128)}, f32[32,32,8,128]{3,2,1,0:T(8,128)}) custom-call(f32[3,2,32,64,256]{4,3,2,1,0:T(8,128)} %field_ref.11, bf16[2,256,512]{2,1,0:T(8,128)(2,1)} %constant.16.clone.refs_0_.refs_16_, bf16[2,256,512]{2,1,0:T(8,128)(2,1)} %constant.17.clone.refs_1_), custom_call_target="tpu_custom_call" | custom-call | flops 6442450944 | bytes 12582912 | tf_op jit(solution)/shard_map/depth_synthesis/pallas_call | solution.py:101
  33.7 77.7 %all-to-all-done = f32[32,32,8,128]{3,2,1,0:T(8,128)} async-done(((f32[32,32,8,128]{3,2,1,0:T(8,128)}), f32[32,32,8,128]{3,2,1,0:T(8,128)}, u32[]{:S(2)}, u32[]{:S(2)}) %all-to-all-start) | async-done | bytes 4194336 | tf_op jit(solution)/shard_map/all_to_all | solution.py:118
  116.8 16.7 %depth_synthesis.6 = (f32[32,32,8,128]{3,2,1,0:T(8,128)}, f32[32,32,8,128]{3,2,1,0:T(8,128)}) custom-call(f32[3,2,32,64,256]{4,3,2,1,0:T(8,128)} %field_ref.11, bf16[2,256,512]{2,1,0:T(8,128)(2,1)} %constant.16.clone.refs_0_.refs_16_, bf16[2,256,512]{2,1,0:T(8,128)(2,1)} %constant.17.clone.refs_1_), custom_call_target="tpu_custom_call" | custom-call | flops 6442450944 | bytes 12582912 | tf_op jit(solution)/shard_map/depth_synthesis/pallas_call | solution.py:101
  146.4 64.8 %all-to-all-done.1 = f32[32,32,8,128]{3,2,1,0:T(8,128)} async-done(((f32[32,32,8,128]{3,2,1,0:T(8,128)}), f32[32,32,8,128]{3,2,1,0:T(8,128)}, u32[]{:S(2)}, u32[]{:S(2)}) %all-to-all-start.1) | async-done | bytes 4194336 | tf_op jit(solution)/shard_map/all_to_all | solution.py:118
  226.2 12.9 %field_lines.7.refs_3_ = f32[8,512,256]{2,1,0:T(8,128)} custom-call(f32[32,256,128]{2,1,0:T(8,128)} %bitcast.1.field.refs_0_, bf16[2,512,512]{2,1,0:T(8,128)(2,1)} %constant.18.clone.span.refs_5_, bf16[2,512,512]{2,1,0:T(8,128)(2,1)} %constant.19.clone.synth.refs_7_), custom_call_target="tpu_custom_call" | custom-call | flops 6442450944 | bytes 8388608 | tf_op jit(solution)/shard_map/field_lines/pallas_call | solution.py:169
  239.1 71.9 %all-to-all-done.2 = f32[32,32,8,128]{3,2,1,0:T(8,128)} async-done(((f32[32,32,8,128]{3,2,1,0:T(8,128)}), f32[32,32,8,128]{3,2,1,0:T(8,128)}, u32[]{:S(2)}, u32[]{:S(2)}) %all-to-all-start.2) | async-done | bytes 4194336 | tf_op jit(solution)/shard_map/all_to_all | solution.py:118
  326.0 13.0 %field_lines.8.refs_4_ = f32[8,512,256]{2,1,0:T(8,128)} custom-call(f32[32,256,128]{2,1,0:T(8,128)} %bitcast.2.field.refs_1_, bf16[2,512,512]{2,1,0:T(8,128)(2,1)} %constant.18.clone.span.refs_5_, bf16[2,512,512]{2,1,0:T(8,128)(2,1)} %constant.19.clone.synth.refs_7_), custom_call_target="tpu_custom_call" | custom-call | flops 6442450944 | bytes 8388608 | tf_op jit(solution)/shard_map/field_lines/pallas_call | solution.py:169
  339.0 71.7 %all-to-all-done.3 = f32[32,32,8,128]{3,2,1,0:T(8,128)} async-done(((f32[32,32,8,128]{3,2,1,0:T(8,128)}), f32[32,32,8,128]{3,2,1,0:T(8,128)}, u32[]{:S(2)}, u32[]{:S(2)}) %all-to-all-start.3) | async-done | bytes 4194336 | tf_op jit(solution)/shard_map/all_to_all | solution.py:118
  426.0 12.9 %field_lines.9.refs_0_ = f32[8,512,256]{2,1,0:T(8,128)} custom-call(f32[32,256,128]{2,1,0:T(8,128)} %bitcast.3.field, bf16[2,512,512]{2,1,0:T(8,128)(2,1)} %constant.18.clone.span.refs_5_, bf16[2,512,512]{2,1,0:T(8,128)(2,1)} %constant.19.clone.synth.refs_7_), custom_call_target="tpu_custom_call" | custom-call | flops 6442450944 | bytes 8388608 | tf_op jit(solution)/shard_map/field_lines/pallas_call | solution.py:169
  438.8 71.7 %all-to-all-done.4 = f32[32,32,8,128]{3,2,1,0:T(8,128)} async-done(((f32[32,32,8,128]{3,2,1,0:T(8,128)}), f32[32,32,8,128]{3,2,1,0:T(8,128)}, u32[]{:S(2)}, u32[]{:S(2)}) %all-to-all-start.4) | async-done | bytes 4194336 | tf_op jit(solution)/shard_map/all_to_all | solution.py:118
  515.9 13.0 %field_lines.10.refs_1_ = f32[8,512,256]{2,1,0:T(8,128)} custom-call(f32[32,256,128]{2,1,0:T(8,128)} %bitcast.4.field, bf16[2,512,512]{2,1,0:T(8,128)(2,1)} %constant.18.clone.span.refs_5_, bf16[2,512,512]{2,1,0:T(8,128)(2,1)} %constant.19.clone.synth.refs_7_), custom_call_target="tpu_custom_call" | custom-call | flops 6442450944 | bytes 8388608 | tf_op jit(solution)/shard_map/field_lines/pallas_call | solution.py:169
  528.9 81.3 %all-to-all-done.5 = f32[32,32,8,128]{3,2,1,0:T(8,128)} async-done(((f32[32,32,8,128]{3,2,1,0:T(8,128)}), f32[32,32,8,128]{3,2,1,0:T(8,128)}, u32[]{:S(2)}, u32[]{:S(2)}) %all-to-all-start.5) | async-done | bytes 4194336 | tf_op jit(solution)/shard_map/all_to_all | solution.py:118
  615.7 12.9 %field_lines.11.refs_2_ = f32[8,512,256]{2,1,0:T(8,128)} custom-call(f32[32,256,128]{2,1,0:T(8,128)} %bitcast.5.field, bf16[2,512,512]{2,1,0:T(8,128)(2,1)} %constant.18.clone.span.refs_5_, bf16[2,512,512]{2,1,0:T(8,128)(2,1)} %constant.19.clone.synth.refs_7_), custom_call_target="tpu_custom_call" | custom-call | flops 6442450944 | bytes 8388608 | tf_op jit(solution)/shard_map/field_lines/pallas_call | solution.py:169
  628.6 21.2 %transport_analysis.1 = (f32[32,8,24,128]{3,2,1,0:T(8,128)}, f32[32,8,24,128]{3,2,1,0:T(8,128)}) custom-call(f32[8,512,256]{2,1,0:T(8,128)} %field_lines.9.refs_0_, f32[8,512,256]{2,1,0:T(8,128)} %field_lines.10.refs_1_, f32[8,512,256]{2,1,0:T(8,128)} %field_lines.11.refs_2_, f32[8,512,256]{2,1,0:T(8,128)} %field_lines.7.refs_3_, ...), custom_call_target="tpu_custom_call" | custom-call | flops 19327352832 | bytes 50331648 | tf_op jit(solution)/shard_map/transport_analysis/pallas_call | solution.py:237
  649.7 60.3 %all-to-all-done.6 = f32[32,32,8,128]{3,2,1,0:T(8,128)} async-done(((f32[32,32,8,128]{3,2,1,0:T(8,128)}), f32[32,32,8,128]{3,2,1,0:T(8,128)}, u32[]{:S(2)}, u32[]{:S(2)}) %all-to-all-start.6) | async-done | bytes 4194336 | tf_op jit(solution)/shard_map/all_to_all | solution.py:118
  710.0 99.0 %all_to_all.65 = f32[32,32,8,128]{3,2,1,0:T(8,128)} all-to-all(f32[32,32,8,128]{3,2,1,0:T(8,128)} %get-tuple-element.82), channel_id=1, replica_groups=mesh['narrow'=4,'wide'=8] {'wide','narrow'}, dimensions={0} | all-to-all | bytes 8388608 | tf_op jit(solution)/shard_map/all_to_all | solution.py:118
  812.8 47.9 %vorticity_lines.1 = (f32[8,512,256]{2,1,0:T(8,128)}, f32[8,512,256]{2,1,0:T(8,128)}, f32[8,512,256]{2,1,0:T(8,128)}) custom-call(f32[32,256,128]{2,1,0:T(8,128)} %bitcast.1.field.refs_0_, f32[32,256,128]{2,1,0:T(8,128)} %bitcast.2.field.refs_1_, f32[32,256,128]{2,1,0:T(8,128)} %bitcast.field.refs_2_, f32[32,256,128]{2,1,0:T(8,128)} %bitcast.6.refs_3_, ...), custom_call_target="tpu_custom_call" | custom-call | flops 19327352832 | bytes 25165824 | tf_op jit(solution)/shard_map/vorticity_lines/pallas_call | solution.py:169
  860.7 23.8 %all-to-all-done.8 = f32[32,8,24,128]{3,2,1,0:T(8,128)S(1)} async-done(((f32[32,8,24,128]{3,2,1,0:T(8,128)}), f32[32,8,24,128]{3,2,1,0:T(8,128)S(1)}, u32[]{:S(2)}, u32[]{:S(2)}) %all-to-all-start.8) | async-done | bytes 3145760 | tf_op jit(solution)/shard_map/all_to_all | solution.py:118
  889.4 40.4 %products_and_analysis.1 = (f32[32,8,24,128]{3,2,1,0:T(8,128)}, f32[32,8,24,128]{3,2,1,0:T(8,128)}, f32[32,8,24,128]{3,2,1,0:T(8,128)}) custom-call(f32[8,512,256]{2,1,0:T(8,128)} %field_lines.9.refs_0_, f32[8,512,256]{2,1,0:T(8,128)} %field_lines.10.refs_1_, f32[8,512,256]{2,1,0:T(8,128)} %field_lines.11.refs_2_, f32[8,512,256]{2,1,0:T(8,128)} %field_lines.7.refs_3_, ...), custom_call_target="tpu_custom_call" | custom-call | flops 28991029248 | bytes 50331648 | tf_op jit(solution)/shard_map/products_and_analysis/pallas_call | solution.py:237
  929.8 31.1 %all-to-all-done.9 = f32[32,8,24,128]{3,2,1,0:T(8,128)} async-done(((f32[32,8,24,128]{3,2,1,0:T(8,128)}), f32[32,8,24,128]{3,2,1,0:T(8,128)}, u32[]{:S(2)}, u32[]{:S(2)}) %all-to-all-start.9) | async-done | bytes 3145760 | tf_op jit(solution)/shard_map/all_to_all | solution.py:118
  960.9 75.8 %all_to_all.66 = f32[32,8,24,128]{3,2,1,0:T(8,128)} all-to-all(f32[32,8,24,128]{3,2,1,0:T(8,128)} %get-tuple-element.97), channel_id=1, replica_groups=mesh['narrow'=4,'wide'=8] {'wide','narrow'}, dimensions={0} | all-to-all | bytes 6291456 | tf_op jit(solution)/shard_map/all_to_all | solution.py:118
  1036.7 74.7 %all_to_all.67 = f32[32,8,24,128]{3,2,1,0:T(8,128)} all-to-all(f32[32,8,24,128]{3,2,1,0:T(8,128)S(1)} %copy-done.1), channel_id=1, replica_groups=mesh['narrow'=4,'wide'=8] {'wide','narrow'}, dimensions={0} | all-to-all | bytes 6291456 | tf_op jit(solution)/shard_map/all_to_all | solution.py:118
  1125.7 61.2 %all-to-all-done.10 = f32[32,8,24,128]{3,2,1,0:T(8,128)} async-done(((f32[32,8,24,128]{3,2,1,0:T(8,128)}), f32[32,8,24,128]{3,2,1,0:T(8,128)}, u32[]{:S(2)}, u32[]{:S(2)}) %all-to-all-start.10) | async-done | bytes 3145760 | tf_op jit(solution)/shard_map/all_to_all | solution.py:118
  1196.8 32.6 %depth_analysis_projection.1 = f32[3,2,2,2,8,64,256]{6,5,4,3,2,1,0:T(8,128)} custom-call(f32[256,3,8,128]{3,2,1,0:T(8,128)} %bitcast.8.refs_0_.refs_5_, f32[256,3,8,128]{3,2,1,0:T(8,128)} %bitcast.40, f32[256,3,8,128]{3,2,1,0:T(8,128)} %bitcast.43, f32[256,3,8,128]{3,2,1,0:T(8,128)} %bitcast.37, f32[256,3,8,128]{3,2,1,0:T(8,128)} %bitcast.12.refs_4_.refs_9_, ...), custom_call_target="tpu_custom_call" | custom-call | flops 16106127360 | bytes 46137344 | tf_op jit(solution)/shard_map/depth_analysis_projection/pallas_call | solution.py:313
  (40 shorter events, 123.9 us)
Async XLA Ops:
  9.6 101.8 %all-to-all-start = ((f32[32,32,8,128]{3,2,1,0:T(8,128)}), f32[32,32,8,128]{3,2,1,0:T(8,128)}, u32[]{:S(2)}, u32[]{:S(2)}) async-start(f32[32,32,8,128]{3,2,1,0:T(8,128)} %depth_synthesis.11), calls=%async_computation | async-start | bytes 8388608 | tf_op jit(solution)/shard_map/all_to_all | solution.py:118
  111.4 99.8 %all-to-all-start.1 = ((f32[32,32,8,128]{3,2,1,0:T(8,128)}), f32[32,32,8,128]{3,2,1,0:T(8,128)}, u32[]{:S(2)}, u32[]{:S(2)}) async-start(f32[32,32,8,128]{3,2,1,0:T(8,128)} %get-tuple-element.59), calls=%async_computation.1 | async-start | bytes 8388608 | tf_op jit(solution)/shard_map/all_to_all | solution.py:118
  211.2 99.8 %all-to-all-start.2 = ((f32[32,32,8,128]{3,2,1,0:T(8,128)}), f32[32,32,8,128]{3,2,1,0:T(8,128)}, u32[]{:S(2)}, u32[]{:S(2)}) async-start(f32[32,32,8,128]{3,2,1,0:T(8,128)} %get-tuple-element.62), calls=%async_computation.2 | async-start | bytes 8388608 | tf_op jit(solution)/shard_map/all_to_all | solution.py:118
  310.9 99.8 %all-to-all-start.3 = ((f32[32,32,8,128]{3,2,1,0:T(8,128)}), f32[32,32,8,128]{3,2,1,0:T(8,128)}, u32[]{:S(2)}, u32[]{:S(2)}) async-start(f32[32,32,8,128]{3,2,1,0:T(8,128)} %depth_synthesis.10), calls=%async_computation.3 | async-start | bytes 8388608 | tf_op jit(solution)/shard_map/all_to_all | solution.py:118
  410.7 99.8 %all-to-all-start.4 = ((f32[32,32,8,128]{3,2,1,0:T(8,128)}), f32[32,32,8,128]{3,2,1,0:T(8,128)}, u32[]{:S(2)}, u32[]{:S(2)}) async-start(f32[32,32,8,128]{3,2,1,0:T(8,128)} %depth_synthesis.9), calls=%async_computation.4 | async-start | bytes 8388608 | tf_op jit(solution)/shard_map/all_to_all | solution.py:118
  510.6 99.7 %all-to-all-start.5 = ((f32[32,32,8,128]{3,2,1,0:T(8,128)}), f32[32,32,8,128]{3,2,1,0:T(8,128)}, u32[]{:S(2)}, u32[]{:S(2)}) async-start(f32[32,32,8,128]{3,2,1,0:T(8,128)} %depth_synthesis.8), calls=%async_computation.5 | async-start | bytes 8388608 | tf_op jit(solution)/shard_map/all_to_all | solution.py:118
  610.3 99.8 %all-to-all-start.6 = ((f32[32,32,8,128]{3,2,1,0:T(8,128)}), f32[32,32,8,128]{3,2,1,0:T(8,128)}, u32[]{:S(2)}, u32[]{:S(2)}) async-start(f32[32,32,8,128]{3,2,1,0:T(8,128)} %get-tuple-element.71), calls=%async_computation.6 | async-start | bytes 8388608 | tf_op jit(solution)/shard_map/all_to_all | solution.py:118
  809.1 75.5 %all-to-all-start.8 = ((f32[32,8,24,128]{3,2,1,0:T(8,128)}), f32[32,8,24,128]{3,2,1,0:T(8,128)S(1)}, u32[]{:S(2)}, u32[]{:S(2)}) async-start(f32[32,8,24,128]{3,2,1,0:T(8,128)} %get-tuple-element.83), calls=%async_computation.8 | async-start | bytes 6291456 | tf_op jit(solution)/shard_map/all_to_all | solution.py:118
  884.5 230.7 %copy-start = (f32[32,8,24,128]{3,2,1,0:T(8,128)}, f32[32,8,24,128]{3,2,1,0:T(8,128)S(1)}, u32[]{:S(2)}) copy-start(f32[32,8,24,128]{3,2,1,0:T(8,128)S(1)} %all-to-all-done.8) | copy-start | bytes 9437188
  884.5 76.4 %all-to-all-start.9 = ((f32[32,8,24,128]{3,2,1,0:T(8,128)}), f32[32,8,24,128]{3,2,1,0:T(8,128)}, u32[]{:S(2)}, u32[]{:S(2)}) async-start(f32[32,8,24,128]{3,2,1,0:T(8,128)} %get-tuple-element.89), calls=%async_computation.9 | async-start | bytes 6291456 | tf_op jit(solution)/shard_map/all_to_all | solution.py:118
  960.9 75.8 %copy-start.1 = (f32[32,8,24,128]{3,2,1,0:T(8,128)S(1)}, f32[32,8,24,128]{3,2,1,0:T(8,128)}, u32[]{:S(2)}) copy-start(f32[32,8,24,128]{3,2,1,0:T(8,128)} %get-tuple-element.98) | copy-start | bytes 9437188
  1111.4 75.5 %all-to-all-start.10 = ((f32[32,8,24,128]{3,2,1,0:T(8,128)}), f32[32,8,24,128]{3,2,1,0:T(8,128)}, u32[]{:S(2)}, u32[]{:S(2)}) async-start(f32[32,8,24,128]{3,2,1,0:T(8,128)} %get-tuple-element.96), calls=%async_computation.10 | async-start | bytes 6291456 | tf_op jit(solution)/shard_map/all_to_all | solution.py:118
  1116.3 75.8 %collective-permute-start.3 = (f32[256,8,128]{2,1,0:T(8,128)}, f32[256,8,128]{2,1,0:T(8,128)S(1)}, u32[]{:S(2)}, u32[]{:S(2)}) collective-permute-start(f32[256,8,128]{2,1,0:T(8,128)} %slice_bitcast_fusion.1), channel_id=1, source_target_pairs={{8,0},{16,24},{9,1},{17,25},{10,2},{18,26},{11,3},{19,27},{12,4},{... | collective-permute-start | bytes 3145736 | tf_op jit(solution)/shard_map/ppermute | solution.py:308
  1119.8 72.3 %collective-permute-start.4 = (f32[256,8,128]{2,1,0:T(8,128)}, f32[256,8,128]{2,1,0:T(8,128)S(1)}, u32[]{:S(2)}, u32[]{:S(2)}) collective-permute-start(f32[256,8,128]{2,1,0:T(8,128)} %slice_bitcast_fusion), channel_id=1, source_target_pairs={{8,0},{16,24},{9,1},{17,25},{10,2},{18,26},{11,3},{19,27},{12,4},{... | collective-permute-start | bytes 3145736 | tf_op jit(solution)/shard_map/ppermute | solution.py:308
  1188.2 4.6 collective-permute-start
  1189.5 5.1 collective-permute-start.1
  1190.8 5.9 collective-permute-start.2
  1192.1 4.6 copy-start.2
  1192.1 4.6 copy-start.3
  1192.8 4.0 copy-start.4
